TPU v7x, 256 devices: a whole 4x4x8 slice. The times are simulated.
256 devices in a mesh: gx: 4 (over y_lo, core), gy: 8 (over z), gz: 8 (over x, y_hi).
Axes of the slice: x: 4, y: 4 (y_hi: 2, y_lo: 2; y = y_hi * 2 + y_lo), z: 8, core: 2. Of those that a mesh axis runs over, the one named last changes fastest.
Arguments:
- design: float32 [64, 256, 1024], P('gx', 'gy', 'gz'), may hold values from 0 to 1
- modes: float32 [2, 3, 64, 256, 1024], P(None, None, 'gx', 'gy', 'gz'), may hold values from -14 to 14
- eigenvalues: float32 [2], replicated, may hold values from 4 to 40
Outputs:
- sensitivity: float32 [2, 64, 256, 1024], P(None, 'gx', 'gy', 'gz')
All inputs are finite; a program needn't handle non-finite values.
Results may differ from a plain program's by a relative error of at most 0.0001.
Values sent between devices are 32-bit elements; how exact they have to be, the bound alone decides.
A program may use at most 128 MiB of HBM per device.

v0:
```python
import math

import jax
import jax.numpy as jnp
import numpy as np
from jax import lax
from jax.sharding import PartitionSpec as P


def with_halo(cells, sides, width):
    for axis, dim in sides:
        count = lax.axis_size(axis)
        ends = count - 1
        head = lax.slice_in_dim(cells, 0, width, axis=dim)
        tail = lax.slice_in_dim(cells, cells.shape[dim] - width, cells.shape[dim], axis=dim)
        cells = jnp.concatenate(
            [
                lax.ppermute(tail, axis, [(i, (i + 1) % count) for i in range(ends)]),
                cells,
                lax.ppermute(head, axis, [((i + 1) % count, i) for i in range(ends)]),
            ],
            axis=dim,
        )
    return cells


def from_behind(value, axis, steps):
    count = lax.axis_size(axis)
    first, last = (max(0, -steps), min(count, count - steps))
    return lax.ppermute(value, axis, [(source, source + steps) for source in range(first, last)])


def offset_table():
    table = []
    for ox in range(-2, 3):
        for oy in range(-2, 3):
            for oz in range(-2, 3):
                radius = math.sqrt(ox * ox + oy * oy + oz * oz)
                if radius < 3.0:
                    table.append((ox, oy, oz, 3.0 - radius))
    return table


def element_tables():
    points = [(1.0 - 1.0 / math.sqrt(3.0)) / 2.0, (1.0 + 1.0 / math.sqrt(3.0)) / 2.0]
    poisson = 0.3
    factor = 1.0 / ((1.0 + poisson) * (1.0 - 2.0 * poisson))
    elastic = np.zeros((6, 6))
    elastic[:3, :3] = poisson * factor
    for i in range(3):
        elastic[i, i] = (1.0 - poisson) * factor
        elastic[3 + i, 3 + i] = (1.0 - 2.0 * poisson) / 2.0 * factor
    stiff = np.zeros((24, 24))
    mass = np.zeros((24, 24))
    for px in points:
        for py in points:
            for pz in points:
                shapes = np.zeros(8)
                grads = np.zeros((8, 3))
                for a in range(2):
                    for b in range(2):
                        for c in range(2):
                            node = 4 * a + 2 * b + c
                            fx = px if a else 1.0 - px
                            fy = py if b else 1.0 - py
                            fz = pz if c else 1.0 - pz
                            dx = 1.0 if a else -1.0
                            dy = 1.0 if b else -1.0
                            dz = 1.0 if c else -1.0
                            shapes[node] = fx * fy * fz
                            grads[node] = [dx * fy * fz, fx * dy * fz, fx * fy * dz]
                strain = np.zeros((6, 24))
                for node in range(8):
                    gxv, gyv, gzv = grads[node]
                    col = 3 * node
                    strain[0, col] = gxv
                    strain[1, col + 1] = gyv
                    strain[2, col + 2] = gzv
                    strain[3, col] = gyv
                    strain[3, col + 1] = gxv
                    strain[4, col + 1] = gzv
                    strain[4, col + 2] = gyv
                    strain[5, col] = gzv
                    strain[5, col + 2] = gxv
                stiff += 0.125 * strain.T @ elastic @ strain
                mass += 0.125 * np.kron(np.outer(shapes, shapes), np.eye(3))
    return np.concatenate([stiff, mass], axis=0).astype(np.float32)


def apply_filter(padded, margin, shape):
    total = None
    for ox, oy, oz, weight in offset_table():
        piece = padded[
            ...,
            margin + ox : margin + ox + shape[0],
            margin + oy : margin + oy + shape[1],
            margin + oz : margin + oz + shape[2],
        ]
        total = weight * piece if total is None else total + weight * piece
    return total


def element_terms(nodes, shape):
    table = jnp.asarray(element_tables()).astype(nodes.dtype)
    slabs = shape[0] // 4

    def slab(start):
        piece = lax.dynamic_slice_in_dim(nodes, start, 5, 2)
        corners = []
        for a in range(2):
            for b in range(2):
                for c in range(2):
                    corners.append(piece[:, :, a : a + 4, b : b + shape[1], c : c + shape[2]])
        stacked = jnp.stack(corners, axis=1)
        vectors = stacked.reshape(stacked.shape[0], 24, 4, shape[1], shape[2])
        images = jnp.einsum("pq,mqxyz->mpxyz", table, vectors, precision=lax.Precision.HIGHEST)
        stiff_term = jnp.sum(vectors * images[:, :24], axis=1)
        mass_term = jnp.sum(vectors * images[:, 24:], axis=1)
        return (stiff_term, mass_term)

    starts = jnp.arange(slabs, dtype=jnp.int32) * 4
    stiff_all, mass_all = lax.map(slab, starts)

    def order(values):
        moved = jnp.moveaxis(values, 0, 1)
        return moved.reshape(moved.shape[0], shape[0], shape[1], shape[2])

    return (order(stiff_all), order(mass_all))


def project(filtered):
    rise = jnp.tanh(8.0 * (filtered - 0.5))
    scale = 2.0 * jnp.tanh(jnp.asarray(4.0, filtered.dtype))
    physical = (jnp.tanh(jnp.asarray(4.0, filtered.dtype)) + rise) / scale
    slope = 8.0 * (1.0 - rise * rise) / scale
    return (physical, slope)


def inside_range(position, count, margin, total):
    cells = position * count - margin + jnp.arange(count + 2 * margin, dtype=jnp.int32)
    return ((cells >= 0) & (cells < total)).astype(jnp.float32)


def domain(margin, shape):
    first = inside_range(lax.axis_index("gx"), shape[0], margin, shape[0] * lax.axis_size("gx"))
    second = inside_range(lax.axis_index("gy"), shape[1], margin, shape[1] * lax.axis_size("gy"))
    third = inside_range(lax.axis_index("gz"), shape[2], margin, shape[2] * lax.axis_size("gz"))
    return first[:, None, None] * second[None, :, None] * third[None, None, :]


def per_device(design, modes, eigenvalues):
    shape = design.shape
    count = float(
        shape[0]
        * lax.axis_size("gx")
        * shape[1]
        * lax.axis_size("gy")
        * shape[2]
        * lax.axis_size("gz")
    )
    padded_design = with_halo(design, (("gx", 0), ("gy", 1), ("gz", 2)), 2)
    weight_sum = apply_filter(domain(2, shape), 2, shape)
    filtered = apply_filter(padded_design, 2, shape) / weight_sum
    physical, slope = project(filtered)
    received = from_behind(modes[:, :, :1], "gx", -1)
    nodes = jnp.concatenate([modes, received], axis=2)
    received = from_behind(nodes[:, :, :, :1], "gy", -1)
    nodes = jnp.concatenate([nodes, received], axis=3)
    received = from_behind(nodes[:, :, :, :, :1], "gz", -1)
    nodes = jnp.concatenate([nodes, received], axis=4)
    stiff_term, mass_term = element_terms(nodes, shape)
    local_mass = jnp.sum(physical[None] * mass_term, axis=(1, 2, 3))
    mass_total = lax.psum(local_mass, ("gx", "gy", "gz"))
    grad = (
        3.0 * (1.0 - 0.001) * physical[None] ** 2 * stiff_term
        - eigenvalues[:, None, None, None] * mass_term
    )
    grad = grad * (slope / weight_sum)[None]
    grad = grad / mass_total[:, None, None, None]
    padded_grad = with_halo(grad, (("gx", 1), ("gy", 2), ("gz", 3)), 2)
    summed = apply_filter(padded_grad, 2, shape)
    return summed * count


def solution(mesh):
    return jax.shard_map(
        per_device,
        mesh=mesh,
        in_specs=(P("gx", "gy", "gz"), P(None, None, "gx", "gy", "gz"), P()),
        out_specs=P(None, "gx", "gy", "gz"),
        check_vma=False,
    )
```

profile of v0, /device:TPU:1, one launch (start us, length us, event | category | flops | bytes accessed | tf_op | source)
XLA Modules:
  0.0 327.6 jit_solution(359366760705941157)
XLA Ops:
  0.8 4.6 %collective-permute-start = (f32[2,32,128]{2,1,0:T(8,128)S(1)}, f32[2,32,128]{2,1,0:T(8,128)S(1)}, u32[]{:S(2)}, u32[]{:S(2)}) collective-permute-start(f32[2,32,128]{2,1,0:T(8,128)S(1)} %get-tuple-element.112), channel_id=1, source_target_pairs={{0,64},{64,128},{128,192},{1,65},{65,129},{129,193},{2,66},{66,130... | collective-permute-start | bytes 98312 | tf_op jit(solution)/shard_map/ppermute | solution.py:18
  11.7 3.5 %collective-permute-start.2 = (f32[20,2,128]{2,1,0:T(2,128)S(1)}, f32[20,2,128]{2,1,0:T(2,128)S(1)}, u32[]{:S(2)}, u32[]{:S(2)}) collective-permute-start(f32[20,2,128]{2,1,0:T(2,128)S(1)} %get-tuple-element.104), channel_id=1, source_target_pairs={{0,8},{8,16},{16,24},{24,32},{32,40},{40,48},{48,56},{1,9},{9,17},... | collective-permute-start | bytes 61448 | tf_op jit(solution)/shard_map/ppermute | solution.py:18
  21.1 4.5 %collective-permute-start.4 = (f32[20,36,2]{2,1,0:T(8,128)}, f32[20,36,2]{2,1,0:T(8,128)S(1)}, u32[]{:S(2)}, u32[]{:S(2)}) collective-permute-start(f32[20,36,2]{2,1,0:T(8,128)} %get-tuple-element.100), channel_id=1, source_target_pairs={{0,1},{1,2},{2,3},{3,4},{4,5},{5,6},{6,7},{8,9},{9,10},{10,11},{11... | collective-permute-start | bytes 17288 | tf_op jit(solution)/shard_map/ppermute | solution.py:18
  27.0 16.4 %collective-permute-done.4 = f32[20,36,2]{2,1,0:T(8,128)S(1)} collective-permute-done((f32[20,36,2]{2,1,0:T(8,128)}, f32[20,36,2]{2,1,0:T(8,128)S(1)}, u32[]{:S(2)}, u32[]{:S(2)}) %collective-permute-start.4) | collective-permute-done | bytes 5792 | tf_op jit(solution)/shard_map/ppermute | solution.py:18
  47.3 11.2 %multiply_multiply_fusion = (f32[16,32,128]{2,1,0:T(8,128)}, f32[16,32,128]{2,1,0:T(8,128)}, f32[16,32,128]{2,1,0:T(8,128)}) fusion(f32[20,2,128]{2,1,0:T(2,128)S(1)} %collective-permute-done.3, f32[20,32,128]{2,1,0:T(8,128)S(1)} %copy-done.2, f32[20,36,130]{2,1,0:T(8,128)S(1)} %get-tuple-element.103, f32[20,36,130]{2,1,0:T(8,128)S(1)} %get-tuple-element.102, ...), kind=kLoop, calls=%fused_computation.639 | loop fusion | flops 25231360 | bytes 44670976 | tf_op jit(solution)/shard_map/mul | solution.py:175
  58.5 6.9 %copy.78 = f32[2,3,17,32,128]{3,0,4,2,1:T(2,128)} copy(f32[2,3,17,32,128]{4,3,2,1,0:T(8,128)S(1)} %constant_dynamic-update-slice_fusion.7) | data formatting | bytes 3342336 | tf_op jit(solution)/shard_map/concatenate | solution.py:166
  65.4 6.8 %copy.79 = f32[2,3,17,1,128]{3,0,4,2,1:T(2,128)} copy(f32[2,3,17,1,128]{4,0,3,2,1:T(2,128)S(1)} %collective-permute-done.7) | data formatting | bytes 104448 | tf_op jit(solution)/shard_map/ppermute | solution.py:30
  75.8 5.2 %collective-permute-done.8 = f32[2,3,17,33,1]{3,0,4,2,1:T(2,128)S(1)} collective-permute-done((f32[2,3,17,33,1]{3,0,4,2,1:T(2,128)S(1)}, f32[2,3,17,33,1]{3,0,4,2,1:T(2,128)S(1)}, u32[]{:S(2)}, u32[]{:S(2)}) %collective-permute-start.8) | collective-permute-done | bytes 13496 | tf_op jit(solution)/shard_map/ppermute | solution.py:30
  81.0 10.4 %pad_maximum_fusion = f32[2,3,17,33,129]{3,0,4,2,1:T(2,128)} fusion(f32[2,3,17,33,1]{3,0,4,2,1:T(2,128)S(1)} %collective-permute-done.8, f32[2,3,17,1,128]{3,0,4,2,1:T(2,128)S(1)} %copy-done, f32[2,3,17,32,128]{3,0,4,2,1:T(2,128)S(1)} %bitcast.93), kind=kLoop, calls=%fused_computation.25 | loop fusion | flops 868428 | bytes 3473712 | tf_op jit(solution)/shard_map/concatenate | solution.py:170
  91.4 11.2 %copy.80 = f32[2,3,17,33,129]{4,3,2,1,0:T(8,128)} copy(f32[2,3,17,33,129]{3,0,4,2,1:T(2,128)} %pad_maximum_fusion) | data formatting | bytes 3473712
  102.7 98.2 %while.13 = (s32[]{:T(128)}, f32[4,2,4,32,128]{4,3,2,1,0:T(8,128)}, f32[4,2,4,32,128]{4,3,2,1,0:T(8,128)}, s32[4]{0:T(128)S(1)}, f32[2,3,17,33,129]{4,3,2,1,0:T(...) while((s32[]{:T(128)}, f32[4,2,4,32,128]{4,3,2,1,0:T(8,128)}, ...), condition=%wide.region_3.4_spmd.clone, body=%wide.region_0.3_spmd.sunk.clone.sunk | while | flops 456065024 | bytes 25957604 | solution.py:122
  115.3 7.4 %fusion.352 = f32[2,48,4,32,128]{4,1,3,2,0:T(8,128)S(1)} fusion(f32[48,24,1,1,1]{0,1,4,3,2:T(8,128)S(1)} %get-tuple-element.182, f32[2,24,4,32,128]{4,3,2,1,0:T(8,128)S(1)} %bitcast.90), kind=kOutput, calls=%fused_computation.6.clone.1 | convolution fusion | flops 452984832 | bytes 9441792 | tf_op jit(solution)/shard_map/while/body/eval_jaxpr/pq,mqxyz->mpxyz/dot_general | solution.py:116
  122.7 4.0 %fusion.353 = (f32[2,4,32,128]{3,2,1,0:T(8,128)S(1)}, f32[2,4,32,128]{3,2,1,0:T(8,128)S(1)}) fusion(f32[2,48,4,32,128]{4,1,3,2,0:T(8,128)S(1)} %fusion.352, f32[2,24,4,32,128]{4,3,2,1,0:T(8,128)S(1)} %bitcast.91), kind=kLoop, calls=%fused_computation.1.clone.1 | loop fusion | flops 3080192 | bytes 9699328 | tf_op jit(solution)/shard_map/while/body/eval_jaxpr/reduce_sum | solution.py:118
  139.8 7.4 %fusion.352 = f32[2,48,4,32,128]{4,1,3,2,0:T(8,128)S(1)} fusion(f32[48,24,1,1,1]{0,1,4,3,2:T(8,128)S(1)} %get-tuple-element.182, f32[2,24,4,32,128]{4,3,2,1,0:T(8,128)S(1)} %bitcast.90), kind=kOutput, calls=%fused_computation.6.clone.1 | convolution fusion | flops 452984832 | bytes 9441792 | tf_op jit(solution)/shard_map/while/body/eval_jaxpr/pq,mqxyz->mpxyz/dot_general | solution.py:116
  147.2 4.0 %fusion.353 = (f32[2,4,32,128]{3,2,1,0:T(8,128)S(1)}, f32[2,4,32,128]{3,2,1,0:T(8,128)S(1)}) fusion(f32[2,48,4,32,128]{4,1,3,2,0:T(8,128)S(1)} %fusion.352, f32[2,24,4,32,128]{4,3,2,1,0:T(8,128)S(1)} %bitcast.91), kind=kLoop, calls=%fused_computation.1.clone.1 | loop fusion | flops 3080192 | bytes 9699328 | tf_op jit(solution)/shard_map/while/body/eval_jaxpr/reduce_sum | solution.py:118
  164.3 7.4 %fusion.352 = f32[2,48,4,32,128]{4,1,3,2,0:T(8,128)S(1)} fusion(f32[48,24,1,1,1]{0,1,4,3,2:T(8,128)S(1)} %get-tuple-element.182, f32[2,24,4,32,128]{4,3,2,1,0:T(8,128)S(1)} %bitcast.90), kind=kOutput, calls=%fused_computation.6.clone.1 | convolution fusion | flops 452984832 | bytes 9441792 | tf_op jit(solution)/shard_map/while/body/eval_jaxpr/pq,mqxyz->mpxyz/dot_general | solution.py:116
  171.7 4.0 %fusion.353 = (f32[2,4,32,128]{3,2,1,0:T(8,128)S(1)}, f32[2,4,32,128]{3,2,1,0:T(8,128)S(1)}) fusion(f32[2,48,4,32,128]{4,1,3,2,0:T(8,128)S(1)} %fusion.352, f32[2,24,4,32,128]{4,3,2,1,0:T(8,128)S(1)} %bitcast.91), kind=kLoop, calls=%fused_computation.1.clone.1 | loop fusion | flops 3080192 | bytes 9699328 | tf_op jit(solution)/shard_map/while/body/eval_jaxpr/reduce_sum | solution.py:118
  188.8 7.4 %fusion.352 = f32[2,48,4,32,128]{4,1,3,2,0:T(8,128)S(1)} fusion(f32[48,24,1,1,1]{0,1,4,3,2:T(8,128)S(1)} %get-tuple-element.182, f32[2,24,4,32,128]{4,3,2,1,0:T(8,128)S(1)} %bitcast.90), kind=kOutput, calls=%fused_computation.6.clone.1 | convolution fusion | flops 452984832 | bytes 9441792 | tf_op jit(solution)/shard_map/while/body/eval_jaxpr/pq,mqxyz->mpxyz/dot_general | solution.py:116
  196.2 4.0 %fusion.353 = (f32[2,4,32,128]{3,2,1,0:T(8,128)S(1)}, f32[2,4,32,128]{3,2,1,0:T(8,128)S(1)}) fusion(f32[2,48,4,32,128]{4,1,3,2,0:T(8,128)S(1)} %fusion.352, f32[2,24,4,32,128]{4,3,2,1,0:T(8,128)S(1)} %bitcast.91), kind=kLoop, calls=%fused_computation.1.clone.1 | loop fusion | flops 3080192 | bytes 9699328 | tf_op jit(solution)/shard_map/while/body/eval_jaxpr/reduce_sum | solution.py:118
  202.2 82.6 %psum.7 = f32[2]{0:T(128)S(1)} all-reduce(f32[2]{0:T(128)S(1)} %multiply_reduce_fusion), channel_id=1, replica_groups=mesh['gx'=4,'gy'=8,'gz'=8] {'gx','gy','gz'}, use_global_device_ids=true, to_apply=%region_5.6 | all-reduce | flops 2 | bytes 16 | tf_op jit(solution)/shard_map/psum | solution.py:173
  295.0 3.6 %collective-permute-start.11 = (f32[2,20,2,128]{3,1,2,0:T(8,128)S(1)}, f32[2,20,2,128]{3,1,2,0:T(8,128)S(1)}, u32[]{:S(2)}, u32[]{:S(2)}) collective-permute-start(f32[2,20,2,128]{3,1,2,0:T(8,128)S(1)} %copy.95), channel_id=1, source_target_pairs={{0,8},{8,16},{16,24},{24,32},{32,40},{40,48},{48,56},{1,9},{9,17},... | collective-permute-start | bytes 122888 | tf_op jit(solution)/shard_map/ppermute | solution.py:18
  300.0 3.8 %collective-permute-done.12 = f32[2,20,2,128]{3,1,2,0:T(8,128)S(1)} collective-permute-done((f32[2,20,2,128]{3,1,2,0:T(8,128)S(1)}, f32[2,20,2,128]{3,1,2,0:T(8,128)S(1)}, u32[]{:S(2)}, u32[]{:S(2)}) %collective-permute-start.12) | collective-permute-done | bytes 40992 | tf_op jit(solution)/shard_map/ppermute | solution.py:20
  309.9 4.5 %collective-permute-done.14 = f32[2,20,36,2]{2,1,3,0:T(8,128)S(1)} collective-permute-done((f32[2,20,36,2]{2,1,3,0:T(8,128)S(1)}, f32[2,20,36,2]{2,1,3,0:T(8,128)S(1)}, u32[]{:S(2)}, u32[]{:S(2)}) %collective-permute-start.14) | collective-permute-done | bytes 11552 | tf_op jit(solution)/shard_map/ppermute | solution.py:20
  317.6 10.0 %fusion.64 = f32[2,16,32,128]{3,2,1,0:T(8,128)} fusion(f32[2,20,34,128]{3,2,1,0:T(8,128)S(1)} %get-tuple-element.95, f32[2,20,36,130]{3,2,1,0:T(8,128)S(1)} %get-tuple-element.93, f32[2,2,32,128]{3,2,1,0:T(8,128)S(1)} %collective-permute-done.10, f32[2,16,32,128]{3,2,1,0:T(8,128)S(1)} %multiply_divide_fusion, f32[2,20,36,130]{3,2,1,0:T(8,128)S(1)} %get-tuple-element.92, ...), kind=kLoop, calls=%fused_computation.123 | loop fusion | flops 24117248 | bytes 47316992 | tf_op jit(solution)/shard_map/mul | solution.py:182
  (134 shorter events, 88.0 us)
Async XLA Ops:
  0.8 9.7 %collective-permute-start = (f32[2,32,128]{2,1,0:T(8,128)S(1)}, f32[2,32,128]{2,1,0:T(8,128)S(1)}, u32[]{:S(2)}, u32[]{:S(2)}) collective-permute-start(f32[2,32,128]{2,1,0:T(8,128)S(1)} %get-tuple-element.112), channel_id=1, source_target_pairs={{0,64},{64,128},{128,192},{1,65},{65,129},{129,193},{2,66},{66,130... | collective-permute-start | bytes 98312 | tf_op jit(solution)/shard_map/ppermute | solution.py:18
  5.4 6.3 %collective-permute-start.1 = (f32[2,32,128]{2,1,0:T(8,128)S(1)}, f32[2,32,128]{2,1,0:T(8,128)S(1)}, u32[]{:S(2)}, u32[]{:S(2)}) collective-permute-start(f32[2,32,128]{2,1,0:T(8,128)S(1)} %get-tuple-element.111), channel_id=1, source_target_pairs={{64,0},{128,64},{192,128},{65,1},{129,65},{193,129},{66,2},{130,66... | collective-permute-start | bytes 98312 | tf_op jit(solution)/shard_map/ppermute | solution.py:20
  8.2 37.7 %collective-permute-start.6 = (f32[2,3,1,32,128]{4,3,2,1,0:T(8,128)S(1)}, f32[2,3,1,32,128]{4,3,2,1,0:T(8,128)S(1)}, u32[]{:S(2)}, u32[]{:S(2)}) collective-permute-start(f32[2,3,1,32,128]{4,3,2,1,0:T(8,128)S(1)} %slice.1281), channel_id=1, source_target_pairs={{64,0},{128,64},{192,128},{65,1},{129,65},{193,129},{66,2},{130,66... | collective-permute-start | bytes 294920 | tf_op jit(solution)/shard_map/ppermute | solution.py:30
  10.2 6.4 %copy-start.5 = (f32[2,3,16,32,128]{4,3,2,1,0:T(8,128)S(1)}, f32[2,3,16,32,128]{4,3,2,1,0:T(8,128)}, u32[]{:S(2)}) copy-start(f32[2,3,16,32,128]{4,3,2,1,0:T(8,128)} %param.7) | copy-start | bytes 4718596
  11.7 31.7 %copy-start.1 = (f32[20,32,128]{2,1,0:T(8,128)}, f32[20,32,128]{2,1,0:T(8,128)S(1)}, u32[]{:S(2)}) copy-start(f32[20,32,128]{2,1,0:T(8,128)S(1)} %get-tuple-element.116) | copy-start | bytes 983044
  11.7 5.0 %collective-permute-start.2 = (f32[20,2,128]{2,1,0:T(2,128)S(1)}, f32[20,2,128]{2,1,0:T(2,128)S(1)}, u32[]{:S(2)}, u32[]{:S(2)}) collective-permute-start(f32[20,2,128]{2,1,0:T(2,128)S(1)} %get-tuple-element.104), channel_id=1, source_target_pairs={{0,8},{8,16},{16,24},{24,32},{32,40},{40,48},{48,56},{1,9},{9,17},... | collective-permute-start | bytes 61448 | tf_op jit(solution)/shard_map/ppermute | solution.py:18
  15.3 4.7 %collective-permute-start.3 = (f32[20,2,128]{2,1,0:T(2,128)S(1)}, f32[20,2,128]{2,1,0:T(2,128)S(1)}, u32[]{:S(2)}, u32[]{:S(2)}) collective-permute-start(f32[20,2,128]{2,1,0:T(2,128)S(1)} %get-tuple-element.105), channel_id=1, source_target_pairs={{8,0},{16,8},{24,16},{32,24},{40,32},{48,40},{56,48},{9,1},{17,9},... | collective-permute-start | bytes 61448 | tf_op jit(solution)/shard_map/ppermute | solution.py:20
  21.1 22.3 %collective-permute-start.4 = (f32[20,36,2]{2,1,0:T(8,128)}, f32[20,36,2]{2,1,0:T(8,128)S(1)}, u32[]{:S(2)}, u32[]{:S(2)}) collective-permute-start(f32[20,36,2]{2,1,0:T(8,128)} %get-tuple-element.100), channel_id=1, source_target_pairs={{0,1},{1,2},{2,3},{3,4},{4,5},{5,6},{6,7},{8,9},{9,10},{10,11},{11... | collective-permute-start | bytes 17288 | tf_op jit(solution)/shard_map/ppermute | solution.py:18
  25.6 18.5 %collective-permute-start.5 = (f32[20,36,2]{2,1,0:T(8,128)}, f32[20,36,2]{2,1,0:T(8,128)}, u32[]{:S(2)}, u32[]{:S(2)}) collective-permute-start(f32[20,36,2]{2,1,0:T(8,128)} %get-tuple-element.101), channel_id=1, source_target_pairs={{1,0},{2,1},{3,2},{4,3},{5,4},{6,5},{7,6},{9,8},{10,9},{11,10},{12... | collective-permute-start | bytes 17288 | tf_op jit(solution)/shard_map/ppermute | solution.py:20
  27.0 20.4 %copy-start.4 = (f32[18,32,128]{2,1,0:T(8,128)S(1)}, f32[18,32,128]{2,1,0:T(8,128)}, u32[]{:S(2)}) copy-start(f32[18,32,128]{2,1,0:T(8,128)} %copy-done.3) | copy-start | bytes 884740
  46.0 19.4 %collective-permute-start.7 = (f32[2,3,17,1,128]{4,0,3,2,1:T(2,128)S(1)}, f32[2,3,17,1,128]{4,0,3,2,1:T(2,128)S(1)}, u32[]{:S(2)}, u32[]{:S(2)}) collective-permute-start(f32[2,3,17,1,128]{4,0,3,2,1:T(2,128)S(1)} %copy.94), channel_id=1, source_target_pairs={{8,0},{16,8},{24,16},{32,24},{40,32},{48,40},{56,48},{9,1},{17,9},... | collective-permute-start | bytes 156680 | tf_op jit(solution)/shard_map/ppermute | solution.py:30
  65.4 15.6 %slice-start = ((s8[6684672]{0:T(1024)(128)(4,1)}), s8[2490368]{0:T(1024)(128)(4,1)S(1)}, s32[]{:S(2)}) async-start(s8[6684672]{0:T(1024)(128)(4,1)} %bitcast.92), calls=%async_computation | async-start | bytes 4980736
  72.2 8.8 %slice-start.1 = ((s8[6684672]{0:T(1024)(128)(4,1)}), s8[4194304]{0:T(1024)(128)(4,1)S(1)}, s32[]{:S(2)}) async-start(s8[6684672]{0:T(1024)(128)(4,1)} %bitcast.92), calls=%async_computation.1 | async-start | bytes 8388608
  72.2 8.8 %copy-start = (f32[2,3,17,1,128]{3,0,4,2,1:T(2,128)S(1)}, f32[2,3,17,1,128]{3,0,4,2,1:T(2,128)}, u32[]{:S(2)}) copy-start(f32[2,3,17,1,128]{3,0,4,2,1:T(2,128)} %copy.79) | copy-start | bytes 156676
  73.4 7.7 %collective-permute-start.8 = (f32[2,3,17,33,1]{3,0,4,2,1:T(2,128)S(1)}, f32[2,3,17,33,1]{3,0,4,2,1:T(2,128)S(1)}, u32[]{:S(2)}, u32[]{:S(2)}) collective-permute-start(f32[2,3,17,33,1]{3,0,4,2,1:T(2,128)S(1)} %pad_maximum_fusion.10), channel_id=1, source_target_pairs={{1,0},{2,1},{3,2},{4,3},{5,4},{6,5},{7,6},{9,8},{10,9},{11,10},{12... | collective-permute-start | bytes 40400 | tf_op jit(solution)/shard_map/ppermute | solution.py:30
  91.4 11.2 %copy-start.11 = (f32[48,24,1,1,1]{0,1,4,3,2:T(8,128)S(1)}, f32[48,24,1,1,1]{0,1,4,3,2:T(8,128)}, u32[]{:S(2)}) copy-start(f32[48,24,1,1,1]{0,1,4,3,2:T(8,128)} %constant.791) | copy-start | bytes 13828
  102.7 184.3 %copy-start.9 = (f32[16,32,128]{2,1,0:T(8,128)S(1)}, f32[16,32,128]{2,1,0:T(8,128)}, u32[]{:S(2)}) copy-start(f32[16,32,128]{2,1,0:T(8,128)} %get-tuple-element.85) | copy-start | bytes 786436
  102.7 184.3 %copy-start.12 = (f32[2]{0:T(128)S(1)}, f32[2]{0:T(128)}, u32[]{:S(2)}) copy-start(f32[2]{0:T(128)} %param.8) | copy-start | bytes 28
  288.1 5.6 %collective-permute-start.10 = (f32[2,2,32,128]{3,2,1,0:T(8,128)S(1)}, f32[2,2,32,128]{3,2,1,0:T(8,128)S(1)}, u32[]{:S(2)}, u32[]{:S(2)}) collective-permute-start(f32[2,2,32,128]{3,2,1,0:T(8,128)S(1)} %get-tuple-element.99), channel_id=1, source_target_pairs={{64,0},{128,64},{192,128},{65,1},{129,65},{193,129},{66,2},{130,66... | collective-permute-start | bytes 196616 | tf_op jit(solution)/shard_map/ppermute | solution.py:20
  291.0 4.0 %collective-permute-start.9 = (f32[2,2,32,128]{3,2,1,0:T(8,128)S(1)}, f32[2,2,32,128]{3,2,1,0:T(8,128)S(1)}, u32[]{:S(2)}, u32[]{:S(2)}) collective-permute-start(f32[2,2,32,128]{3,2,1,0:T(8,128)S(1)} %get-tuple-element.98), channel_id=1, source_target_pairs={{0,64},{64,128},{128,192},{1,65},{65,129},{129,193},{2,66},{66,130... | collective-permute-start | bytes 196616 | tf_op jit(solution)/shard_map/ppermute | solution.py:18
  295.0 4.9 %collective-permute-start.11 = (f32[2,20,2,128]{3,1,2,0:T(8,128)S(1)}, f32[2,20,2,128]{3,1,2,0:T(8,128)S(1)}, u32[]{:S(2)}, u32[]{:S(2)}) collective-permute-start(f32[2,20,2,128]{3,1,2,0:T(8,128)S(1)} %copy.95), channel_id=1, source_target_pairs={{0,8},{8,16},{16,24},{24,32},{32,40},{40,48},{48,56},{1,9},{9,17},... | collective-permute-start | bytes 122888 | tf_op jit(solution)/shard_map/ppermute | solution.py:18
  298.6 5.2 %collective-permute-start.12 = (f32[2,20,2,128]{3,1,2,0:T(8,128)S(1)}, f32[2,20,2,128]{3,1,2,0:T(8,128)S(1)}, u32[]{:S(2)}, u32[]{:S(2)}) collective-permute-start(f32[2,20,2,128]{3,1,2,0:T(8,128)S(1)} %copy.96), channel_id=1, source_target_pairs={{8,0},{16,8},{24,16},{32,24},{40,32},{48,40},{56,48},{9,1},{17,9},... | collective-permute-start | bytes 122888 | tf_op jit(solution)/shard_map/ppermute | solution.py:20
  304.6 4.9 %collective-permute-start.13 = (f32[2,20,36,2]{2,1,3,0:T(8,128)S(1)}, f32[2,20,36,2]{2,1,3,0:T(8,128)S(1)}, u32[]{:S(2)}, u32[]{:S(2)}) collective-permute-start(f32[2,20,36,2]{2,1,3,0:T(8,128)S(1)} %copy.88), channel_id=1, source_target_pairs={{0,1},{1,2},{2,3},{3,4},{4,5},{5,6},{6,7},{8,9},{9,10},{10,11},{11... | collective-permute-start | bytes 34568 | tf_op jit(solution)/shard_map/ppermute | solution.py:18
  308.1 6.3 %collective-permute-start.14 = (f32[2,20,36,2]{2,1,3,0:T(8,128)S(1)}, f32[2,20,36,2]{2,1,3,0:T(8,128)S(1)}, u32[]{:S(2)}, u32[]{:S(2)}) collective-permute-start(f32[2,20,36,2]{2,1,3,0:T(8,128)S(1)} %copy.90), channel_id=1, source_target_pairs={{1,0},{2,1},{3,2},{4,3},{5,4},{6,5},{7,6},{9,8},{10,9},{11,10},{12... | collective-permute-start | bytes 34568 | tf_op jit(solution)/shard_map/ppermute | solution.py:20
  (6 other events, 18.1 us)
where the time goes:
time: 333 us; the launch traced here: 328 us
  blocking collectives  82.6 us (25%)
  local copies, waits for them, and re-layouts  79.3 us (24%)
  other arithmetic  56.1 us (17%)
  starting transfers between devices  36.7 us (11%)
  waiting for transfers between devices  34.4 us (10%)
  matrix products  29.6 us (9%)
  loops' own time  8.48 us (3%)
    psum x1, blocking collectives, per_device(): mass_total = lax.psum(local_mass, ('gx', 'gy', 'gz'))  82.6 us
    while x28, local copies, waits for them, and re-layouts  33.3 us
    dot_general x4, matrix products, slab(): jnp.einsum('pq,mqxyz->mpxyz', table, vectors, precision=lax.Precision.HIG...  29.6 us
    ppermute x6, starting transfers between devices, with_halo(): lax.ppermute(tail, axis, [(i, (i + 1) % count) for i in range(ends)])  21.9 us
    ppermute x6, waiting for transfers between devices, with_halo(): lax.ppermute(tail, axis, [(i, (i + 1) % count) for i in range(ends)])  17.7 us
    reduce_sum x4, other arithmetic, slab(): mass_term = jnp.sum(vectors * images[:, 24:], axis=1)  15.9 us
    unnamed x36, local copies, waits for them, and re-layouts  12.3 us
    ppermute x6, waiting for transfers between devices, with_halo(): lax.ppermute(head, axis, [((i + 1) % count, i) for i in range(ends)])  11.5 us
  transfers between devices with their start and end apart: 15, of which 6 were waited for; matrix products, arithmetic and copies ran while one was open for 8% of the time, Pallas kernels for 0%

commit v1 on v0

v1 whole, which is shorter than its diff:
```python
import itertools
import math

import jax
import jax.numpy as jnp
from jax import lax
from jax.experimental import pallas as pl
from jax.experimental.pallas import tpu as pltpu
from jax.sharding import PartitionSpec as P

AXES = ("gx", "gy", "gz")
MESH = pl.DeviceIdType.MESH
TX, TY, TZ = 16, 32, 128
NEAR = [o for o in itertools.product((-1, 0, 1), repeat=3) if o != (0, 0, 0)]
FLAT = [o for o in NEAR if o[2] == 0]
F32 = jnp.float32


def weight(i, j, k):
    return max(0.0, 3.0 - math.sqrt(i * i + j * j + k * k))


def column(dx, dy):
    return (dx + 1) * 3 + (dy + 1)


X_SPAN = {-1: (0, TX + 2, 2), 0: (0, 2, TX), 1: (TX - 2, 0, 2)}
Y_SPAN = {-1: (0, TY + 8, 2), 0: (0, 8, TY), 1: (TY - 2, 6, 2)}


def combine(a, weights):
    total = None
    for value, w in zip(a, weights):
        if w == 0.0:
            continue
        total = w * value if total is None else total + w * value
    return total


def kernel(
    sizes,
    design_ref,
    modes_ref,
    eig_ref,
    raw_ref,
    total_ref,
    dp,
    mb,
    mz,
    zl,
    zh,
    from_hi,
    from_lo,
    sz,
    phys,
    slope,
    gp,
    gl,
    gh,
    g_from_hi,
    g_from_lo,
    outs,
    a_in,
    b_in,
    local_sem,
    out_sem,
    d_send,
    d_recv,
    m_send,
    m_recv,
    g_send,
    g_recv,
    a_send,
    a_recv,
    b_send,
    b_recv,
):
    cx, cy, cz = sizes
    me = tuple(lax.axis_index(a) for a in AXES)
    mx, my, mzi = me

    def near(o):
        return tuple(lax.rem(m + (d + s), s) for m, d, s in zip(me, o, sizes))

    a_count, b_count = (cx // 2) * cz, 2 * cy
    a_slot = (mx // 2) * cz + mzi
    b_slot = lax.rem(mx, 2) * cy + my

    def a_device(k):
        slot = lax.rem(a_slot + k, a_count)
        return ((slot // cz) * 2 + lax.rem(mx, 2), my, lax.rem(slot, cz))

    def b_device(k):
        slot = lax.rem(b_slot + k, b_count)
        return ((mx // 2) * 2 + slot // cy, lax.rem(slot, cy), mzi)

    barrier = pltpu.get_barrier_semaphore()
    for o in NEAR:
        pl.semaphore_signal(barrier, inc=1, device_id=near(o), device_id_type=MESH)
    for k in range(1, a_count):
        pl.semaphore_signal(barrier, inc=1, device_id=a_device(k), device_id_type=MESH)
    for k in range(1, b_count):
        pl.semaphore_signal(barrier, inc=1, device_id=b_device(k), device_id_type=MESH)

    load_design = pltpu.make_async_copy(
        design_ref, dp.at[pl.ds(2, TX), pl.ds(8, TY)], local_sem.at[0]
    )
    load_design.start()
    load_modes = pltpu.make_async_copy(
        modes_ref, mb.at[:, pl.ds(0, TX), pl.ds(0, TY)], local_sem.at[1]
    )
    load_modes.start()

    lane = lax.broadcasted_iota(jnp.int32, (8, 128), 1)
    pair = lax.shift_right_logical(lane, 1)
    zero = jnp.zeros((8, 128), F32)

    load_design.wait()

    def pack_design(x, carry):
        lo, hi = carry
        for g in range(4):
            k = 4 * x + g
            r = pltpu.roll(dp[x + 2, 8 + 8 * g : 16 + 8 * g, :], 2 * k, 1)
            lo = jnp.where(pair == k, r, lo)
            hi = jnp.where(pair == lax.rem(k + 63, 64), r, hi)
        return lo, hi

    lo, hi = lax.fori_loop(0, TX, pack_design, (zero, zero))
    zl[0] = lo
    zh[0] = hi

    load_modes.wait()

    def pack_modes(x, carry):
        carry = list(carry)
        for c in range(6):
            for g in range(4):
                k = (c % 2) * 64 + 4 * x + g
                r = pltpu.roll(mb[c, x, 8 * g : 8 * g + 8, :], k, 1)
                carry[c // 2] = jnp.where(lane == k, r, carry[c // 2])
        return tuple(carry)

    packed = lax.fori_loop(0, TX, pack_modes, (zero, zero, zero))
    for i in range(3):
        zl[1 + i] = packed[i]

    pl.semaphore_wait(barrier, len(NEAR) + a_count - 1 + b_count - 1)

    d_copies, m_copies = [], []

    def send(o, src, dst, copies, send_sems, recv_sems):
        i = len(copies)
        copy = pltpu.make_async_remote_copy(
            src_ref=src,
            dst_ref=dst,
            send_sem=send_sems.at[i],
            recv_sem=recv_sems.at[i],
            device_id=near(o),
            device_id_type=MESH,
        )
        copy.start()
        copies.append(copy)

    for o in NEAR:
        dx, dy, dz = o
        if dz == 0:
            (xs, xd, xn), (ys, yd, yn) = X_SPAN[dx], Y_SPAN[dy]
            src = design_ref.at[pl.ds(xs, xn), pl.ds(ys, yn)]
            dst = dp.at[pl.ds(xd, xn), pl.ds(yd, yn)]
        elif dz == 1:
            src, dst = zh, from_lo.at[column(-dx, -dy)]
        elif dx <= 0 and dy <= 0:
            src, dst = zl, from_hi.at[column(-dx, -dy)]
        else:
            src = zl.at[pl.ds(0, 1)]
            dst = from_hi.at[column(-dx, -dy), pl.ds(0, 1)]
        send(o, src, dst, d_copies, d_send, d_recv)
    for o in ((-1, 0, 0), (0, -1, 0), (-1, -1, 0)):
        dx, dy, _ = o
        xs = pl.ds(0, 1) if dx else pl.ds(0, TX)
        xd = pl.ds(TX, 1) if dx else pl.ds(0, TX)
        ys = pl.ds(0, 1) if dy else pl.ds(0, TY)
        yd = pl.ds(TY, 1) if dy else pl.ds(0, TY)
        send(o, modes_ref.at[:, xs, ys], mb.at[:, xd, yd], m_copies, m_send, m_recv)

    def inside(cell, total):
        return ((cell >= 0) & (cell < total)).astype(F32)

    zpos = mzi * TZ + lax.broadcasted_iota(jnp.int32, (8, 128), 1)
    z1 = inside(zpos - 1, cz * TZ) + inside(zpos + 1, cz * TZ)
    z2 = inside(zpos - 2, cz * TZ) + inside(zpos + 2, cz * TZ)
    parts = []
    for g in range(4):
        ypos = my * TY + 8 * g + lax.broadcasted_iota(jnp.int32, (8, 128), 0)
        y1 = inside(ypos - 1, cy * TY) + inside(ypos + 1, cy * TY)
        y2 = inside(ypos - 2, cy * TY) + inside(ypos + 2, cy * TY)
        row = []
        for i in range(3):
            rows = [
                weight(i, j, 0) + weight(i, j, 1) * z1 + weight(i, j, 2) * z2 for j in range(3)
            ]
            row.append(rows[0] + y1 * rows[1] + y2 * rows[2])
        parts.append(row)

    x_lo = (mx > 0).astype(F32)
    x_hi = (mx < cx - 1).astype(F32)
    y_lo = (my > 0).astype(F32)
    y_hi = (my < cy - 1).astype(F32)
    z_lo = (mzi > 0).astype(F32)
    z_hi = (mzi < cz - 1).astype(F32)

    def clear_halo(ref, lead):
        @pl.when(mx == 0)
        def _():
            ref[lead + (slice(0, 2),)] = jnp.zeros_like(ref[lead + (slice(0, 2),)])

        @pl.when(mx == cx - 1)
        def _():
            ref[lead + (slice(TX + 2, TX + 4),)] = jnp.zeros_like(
                ref[lead + (slice(TX + 2, TX + 4),)]
            )

        @pl.when(my == 0)
        def _():
            ref[lead + (slice(None), slice(0, 8))] = jnp.zeros_like(
                ref[lead + (slice(None), slice(0, 8))]
            )

        @pl.when(my == cy - 1)
        def _():
            ref[lead + (slice(None), slice(TY + 8, TY + 16))] = jnp.zeros_like(
                ref[lead + (slice(None), slice(TY + 8, TY + 16))]
            )

    def spread(load, hi_of, lo_of):
        def body(p, _):
            cxi = (p + 14) // 16
            xs = lax.rem(p + 14, 16)
            xmask = jnp.where(cxi == 0, x_lo, jnp.where(cxi == 2, x_hi, 1.0))
            for g in range(6):
                cyi = 0 if g == 0 else 2 if g == 5 else 1
                ys = 3 if g == 0 else 0 if g == 5 else g - 1
                mask = xmask * (y_lo if g == 0 else y_hi if g == 5 else 1.0)
                k = 4 * xs + ys
                back = lax.rem(128 - 2 * k, 128)
                n = cxi * 3 + cyi
                v = load(p, g)
                h_hi = pltpu.roll(hi_of(n), back, 1) * (mask * z_hi)
                h_lo = pltpu.roll(lo_of(n), back, 1) * (mask * z_lo)
                up = jnp.where(lane < 1, h_hi, v)
                down = jnp.where(lane >= 127, h_lo, v)
                up2 = jnp.where(lane < 2, h_hi, v)
                down2 = jnp.where(lane >= 126, h_lo, v)
                rows = slice(8 * g, 8 * g + 8)
                sz[0, p, rows, :] = pltpu.roll(up, 127, 1) + pltpu.roll(down, 1, 1)
                sz[1, p, rows, :] = pltpu.roll(up2, 126, 1) + pltpu.roll(down2, 2, 1)
            return 0

        lax.fori_loop(0, TX + 4, body, 0)

    order = ((0, 0), (0, 1), (1, 1), (0, 2), (1, 2), (2, 2))

    def filtered(load, store):
        def body(p, carry):
            new = []
            for g in range(4):
                terms = {}
                for k in range(3):
                    ref = load if k == 0 else (lambda q, a, b, k=k: sz[k - 1, q, a:b, :])
                    top = 8 + 8 * g
                    terms[0, k] = ref(p, top, top + 8)
                    terms[1, k] = ref(p, top - 1, top + 7) + ref(p, top + 1, top + 9)
                    terms[2, k] = ref(p, top - 2, top + 6) + ref(p, top + 2, top + 10)
                grouped = [
                    terms[i, j] if i == j else terms[i, j] + terms[j, i] for i, j in order
                ]
                f = [
                    combine(grouped, [weight(i, j, k) for j, k in order]) for i in range(3)
                ]
                a0, a1, a2, a3 = carry[4 * g : 4 * g + 4]
                store(p, g, a0 + f[2])
                new += [a1 + f[1], a2 + f[0], a3 + f[1], f[2]]
            return tuple(new)

        lax.fori_loop(0, TX + 4, body, (zero,) * 16)

    for copy in d_copies:
        copy.wait_recv()
    clear_halo(dp, ())
    spread(
        lambda p, g: dp[p, 8 * g : 8 * g + 8, :],
        lambda n: from_hi[n, 0],
        lambda n: from_lo[n, 0],
    )

    top_t = math.tanh(4.0)

    def project(p, g, value):
        xpos = mx * TX + p - 4
        x1 = inside(xpos - 1, cx * TX) + inside(xpos + 1, cx * TX)
        x2 = inside(xpos - 2, cx * TX) + inside(xpos + 2, cx * TX)
        inverse = 1.0 / (parts[g][0] + x1 * parts[g][1] + x2 * parts[g][2])
        t = jnp.tanh(8.0 * (value * inverse - 0.5))
        rows = slice(8 * g, 8 * g + 8)
        phys[p, rows, :] = (top_t + t) * (0.5 / top_t)
        slope[p, rows, :] = (1.0 - t * t) * inverse * (4.0 / top_t)

    filtered(lambda p, a, b: dp[p, a:b, :], project)

    for copy in m_copies:
        copy.wait_recv()

    @pl.when(mx == cx - 1)
    def _():
        mb[:, TX] = jnp.zeros_like(mb[:, TX])

    @pl.when(my == cy - 1)
    def _():
        mb[:, :, TY : TY + 8] = jnp.zeros_like(mb[:, :, TY : TY + 8])

    def shift_modes(x, _):
        cxi = x // 16
        xs = lax.rem(x, 16)
        xmask = jnp.where(cxi == 1, x_hi, 1.0) * z_hi
        for c in range(6):
            for g in range(5):
                ys = g % 4
                k = (c % 2) * 64 + 4 * xs + ys
                n = (cxi + 1) * 3 + 1 + g // 4
                mask = xmask * (y_hi if g == 4 else 1.0)
                h = pltpu.roll(from_hi[n, 1 + c // 2], lax.rem(128 - k, 128), 1) * mask
                v = jnp.where(lane == 0, h, mb[c, x, 8 * g : 8 * g + 8, :])
                mz[c, x, 8 * g : 8 * g + 8, :] = pltpu.roll(v, 127, 1)
        return 0

    lax.fori_loop(0, TX + 1, shift_modes, 0)

    factor = 1.0 / (1.3 * 0.4)
    lam, mu = 0.3 * factor, 0.2 * factor

    def plane(c, x, g):
        a, b = 8 * g, 8 * g + 8
        v0, v1 = mb[c, x, a:b, :], mb[c, x, a + 1 : b + 1, :]
        w0, w1 = mz[c, x, a:b, :], mz[c, x, a + 1 : b + 1, :]
        vs, vd, ws, wd = v0 + v1, v1 - v0, w0 + w1, w1 - w0
        return vs + ws, ws - vs, vd + wd, wd - vd

    def energies(now, later):
        a = {}
        for c in range(3):
            for q, (j, k) in enumerate(((0, 0), (0, 1), (1, 0), (1, 1))):
                a[c, 0, j, k] = now[4 * c + q] + later[4 * c + q]
                a[c, 1, j, k] = later[4 * c + q] - now[4 * c + q]
        s = {key: v * v for key, v in a.items()}

        def sq(v):
            return v * v

        q0 = s[0, 0, 0, 0] + s[1, 0, 0, 0] + s[2, 0, 0, 0]
        axial = s[0, 1, 0, 0] + s[1, 0, 1, 0] + s[2, 0, 0, 1]
        q1 = axial + (
            (s[0, 0, 1, 0] + s[0, 0, 0, 1])
            + (s[1, 1, 0, 0] + s[1, 0, 0, 1])
            + (s[2, 1, 0, 0] + s[2, 0, 1, 0])
        )
        bend = (
            (s[0, 1, 1, 0] + s[0, 1, 0, 1])
            + (s[1, 1, 1, 0] + s[1, 0, 1, 1])
            + (s[2, 1, 0, 1] + s[2, 0, 1, 1])
        )
        q2 = bend + (s[0, 0, 1, 1] + s[1, 1, 0, 1] + s[2, 1, 1, 0])
        q3 = s[0, 1, 1, 1] + s[1, 1, 1, 1] + s[2, 1, 1, 1]
        mass = (1 / 64) * q0 + (1 / 192) * q1 + ((1 / 576) * q2 + (1 / 1728) * q3)
        trace = sq(a[0, 1, 0, 0] + a[1, 0, 1, 0] + a[2, 0, 0, 1])
        shear = (
            sq(a[0, 0, 1, 0] + a[1, 1, 0, 0])
            + sq(a[1, 0, 0, 1] + a[2, 0, 1, 0])
            + sq(a[0, 0, 0, 1] + a[2, 1, 0, 0])
        )
        trace_1 = (
            sq(a[0, 1, 1, 0] + a[2, 0, 1, 1])
            + sq(a[0, 1, 0, 1] + a[1, 0, 1, 1])
            + sq(a[1, 1, 1, 0] + a[2, 1, 0, 1])
        )
        shear_1 = (
            sq(a[0, 0, 1, 1] + a[1, 1, 0, 1])
            + sq(a[1, 1, 0, 1] + a[2, 1, 1, 0])
            + sq(a[0, 0, 1, 1] + a[2, 1, 1, 0])
        )
        stiff = (
            ((lam / 16) * trace + (mu / 8) * axial)
            + ((mu / 16) * shear + (lam / 48) * trace_1)
            + ((mu / 16) * bend + (mu / 48) * shear_1)
            + ((lam + 4 * mu) / 144) * q3
        )
        return stiff, mass

    packs = []
    masses = []
    for m in range(2):
        eig = eig_ref[m]
        lo, hi, acc = zero, zero, zero
        for pairs in range(2):
            groups = (2 * pairs, 2 * pairs + 1)

            def body(x, carry, m=m, groups=groups, eig=eig):
                lo, hi, acc = carry[:3]
                held = carry[3:]
                nexts = []
                for i, g in enumerate(groups):
                    now = held[12 * i : 12 * i + 12]
                    later = sum((plane(3 * m + c, x + 1, g) for c in range(3)), ())
                    nexts += later
                    stiff, mass = energies(now, later)
                    rows = slice(8 * g, 8 * g + 8)
                    rho = phys[x + 4, rows, :]
                    acc = acc + rho * mass
                    grad = ((3.0 * (1.0 - 0.001)) * (rho * rho) * stiff - eig * mass) * slope[
                        x + 4, rows, :
                    ]
                    gp[m, x + 2, 8 + 8 * g : 16 + 8 * g, :] = grad
                    k = 4 * x + g
                    r = pltpu.roll(grad, 2 * k, 1)
                    lo = jnp.where(pair == k, r, lo)
                    hi = jnp.where(pair == lax.rem(k + 63, 64), r, hi)
                return (lo, hi, acc, *nexts)

            first = []
            for g in groups:
                first += sum((plane(3 * m + c, 0, g) for c in range(3)), ())
            lo, hi, acc = lax.fori_loop(0, TX, body, (lo, hi, acc, *first))[:3]
        packs.append((lo, hi))
        masses.append(acc)
    for m in range(2):
        gl[m] = packs[m][0]
        gh[m] = packs[m][1]
        a_in[0, m : m + 1, :] = jnp.sum(masses[m], axis=0, keepdims=True)

    a_copies = []
    for k in range(1, a_count):
        copy = pltpu.make_async_remote_copy(
            src_ref=a_in.at[0],
            dst_ref=a_in.at[k],
            send_sem=a_send.at[k],
            recv_sem=a_recv.at[k],
            device_id=a_device(k),
            device_id_type=MESH,
        )
        copy.start()
        a_copies.append(copy)

    g_copies = []
    for o in NEAR:
        dx, dy, dz = o
        if dz == 0:
            (xs, xd, xn), (ys, yd, yn) = X_SPAN[dx], Y_SPAN[dy]
            src = gp.at[:, pl.ds(xs + 2, xn), pl.ds(ys + 8, yn)]
            dst = gp.at[:, pl.ds(xd, xn), pl.ds(yd, yn)]
        elif dz == 1:
            src, dst = gh, g_from_lo.at[column(-dx, -dy)]
        else:
            src, dst = gl, g_from_hi.at[column(-dx, -dy)]
        send(o, src, dst, g_copies, g_send, g_recv)

    for copy in a_copies:
        copy.wait_recv()
    b_in[0] = jnp.sum(a_in[...], axis=0)
    b_copies = []
    for k in range(1, b_count):
        copy = pltpu.make_async_remote_copy(
            src_ref=b_in.at[0],
            dst_ref=b_in.at[k],
            send_sem=b_send.at[k],
            recv_sem=b_recv.at[k],
            device_id=b_device(k),
            device_id_type=MESH,
        )
        copy.start()
        b_copies.append(copy)

    for copy in g_copies:
        copy.wait_recv()
    clear_halo(gp, (slice(None),))
    stores = []
    for m in range(2):
        spread(
            lambda p, g, m=m: gp[m, p, 8 * g : 8 * g + 8, :],
            lambda n, m=m: g_from_hi[n, m],
            lambda n, m=m: g_from_lo[n, m],
        )

        def keep(p, g, value, m=m):
            outs[m, p, 8 * g : 8 * g + 8, :] = value

        filtered(lambda p, a, b, m=m: gp[m, p, a:b, :], keep)
        store = pltpu.make_async_copy(
            outs.at[m, pl.ds(4, TX)], raw_ref.at[m], out_sem.at[m]
        )
        store.start()
        stores.append(store)

    for copy in b_copies:
        copy.wait_recv()
    total = jnp.sum(jnp.sum(b_in[...], axis=0), axis=1, keepdims=True)
    total_ref[...] = jnp.broadcast_to(total, (2, 128))

    for copy in d_copies + m_copies + a_copies + g_copies + b_copies:
        copy.wait_send()
    for store in stores:
        store.wait()


def per_device(sizes, design, modes, eigenvalues):
    cx, cy, cz = sizes
    a_count, b_count = (cx // 2) * cz, 2 * cy
    count = float(cx * TX * cy * TY * cz * TZ)
    dma = pltpu.SemaphoreType.DMA

    def vmem(*shape):
        return pltpu.VMEM(shape, F32)

    raw, total = pl.pallas_call(
        lambda *refs: kernel(sizes, *refs),
        out_shape=(
            jax.ShapeDtypeStruct((2, TX, TY, TZ), F32),
            jax.ShapeDtypeStruct((2, 128), F32),
        ),
        in_specs=[
            pl.BlockSpec(memory_space=pl.ANY),
            pl.BlockSpec(memory_space=pl.ANY),
            pl.BlockSpec(memory_space=pltpu.SMEM),
        ],
        out_specs=(
            pl.BlockSpec(memory_space=pl.ANY),
            pl.BlockSpec(memory_space=pltpu.VMEM),
        ),
        scratch_shapes=[
            vmem(TX + 4, TY + 16, TZ),
            vmem(6, TX + 1, TY + 8, TZ),
            vmem(6, TX + 1, TY + 8, TZ),
            vmem(4, 8, 128),
            vmem(1, 8, 128),
            vmem(9, 4, 8, 128),
            vmem(9, 1, 8, 128),
            vmem(2, TX + 4, TY + 16, TZ),
            vmem(TX + 4, TY, TZ),
            vmem(TX + 4, TY, TZ),
            vmem(2, TX + 4, TY + 16, TZ),
            vmem(2, 8, 128),
            vmem(2, 8, 128),
            vmem(9, 2, 8, 128),
            vmem(9, 2, 8, 128),
            vmem(2, TX + 4, TY, TZ),
            vmem(a_count, 2, 128),
            vmem(b_count, 2, 128),
            dma((2,)),
            dma((2,)),
            dma((26,)),
            dma((26,)),
            dma((3,)),
            dma((3,)),
            dma((26,)),
            dma((26,)),
            dma((a_count,)),
            dma((a_count,)),
            dma((b_count,)),
            dma((b_count,)),
        ],
        compiler_params=pltpu.CompilerParams(
            collective_id=0, has_side_effects=True, vmem_limit_bytes=40 * 1024 * 1024
        ),
    )(design, modes.reshape(6, TX, TY, TZ), eigenvalues)
    return raw * (count / total[:, 0])[:, None, None, None]


def solution(mesh):
    sizes = tuple(mesh.shape[a] for a in AXES)
    return jax.shard_map(
        lambda design, modes, eigenvalues: per_device(sizes, design, modes, eigenvalues),
        mesh=mesh,
        in_specs=(P("gx", "gy", "gz"), P(None, None, "gx", "gy", "gz"), P()),
        out_specs=P(None, "gx", "gy", "gz"),
        check_vma=False,
    )
```

time: 333 us -> 54.4 us (0.16); the launches traced: 328 us -> 54.3 us
  blocking collectives: 82.6 us -> 0 us
  local copies, waits for them, and re-layouts: 79.3 us -> 3.01 us
  other arithmetic: 56.1 us -> 1.05 us
  Pallas kernels: 0 us -> 50.2 us
  starting transfers between devices: 36.7 us -> 0 us
  waiting for transfers between devices: 34.4 us -> 0 us
  matrix products: 29.6 us -> 0 us
  loops' own time: 8.48 us -> 0 us
    psum x1 -> x0, blocking collectives: 82.6 us -> none  [per_device(): mass_total = lax.psum(local_mass, ('gx', 'gy', 'gz'))]
    pallas_call x0 -> x1, Pallas kernels: none -> 50.2 us  [per_device(): pl.pallas_call(lambda *refs: kernel(sizes, *refs), out_shape=(jax.ShapeDt...]
    ppermute x15 -> x0, starting transfers between devices: 36.7 us -> none  [the longest x6 21.9 us: with_halo(): lax.ppermute(tail, axis, [(i, (i + 1) % count) for i in range(ends)])]
    ppermute x15 -> x0, waiting for transfers between devices: 34.4 us -> none  [the longest x6 17.7 us: with_halo(): lax.ppermute(tail, axis, [(i, (i + 1) % count) for i in range(ends)])]
    while x28 -> x0, local copies, waits for them, and re-layouts: 33.3 us -> none
    dot_general x4 -> x0, matrix products: 29.6 us -> none  [slab(): jnp.einsum('pq,mqxyz->mpxyz', table, vectors, precision=lax.Precision.HIG...]
    mul x5 -> x1, other arithmetic: 21.5 us -> 0.93 us  [per_device(): return raw * (count / total[:, 0])[:, None, None, None]]
    reduce_sum x5 -> x0, other arithmetic: 17.2 us -> none  [the longest x4 15.9 us: slab(): mass_term = jnp.sum(vectors * images[:, 24:], axis=1)]
  transfers between devices with their start and end apart: 15 -> 0, of which waited for: 6 -> 0; matrix products, arithmetic and copies ran while one was open for 8% -> 0% of each run, Pallas kernels for 0% -> 0%
where the time goes in v1:
time: 54.4 us; the launch traced here: 54.3 us
  Pallas kernels  50.2 us (92%)
  local copies, waits for them, and re-layouts  3.01 us (6%)
  other arithmetic  1.05 us (2%)
    pallas_call x1, Pallas kernels, per_device(): pl.pallas_call(lambda *refs: kernel(sizes, *refs), out_shape=(jax.ShapeDt...  50.2 us
    unnamed x6, local copies, waits for them, and re-layouts  3.01 us

profile of v1, /device:TPU:1, one launch (start us, length us, event | category | flops | bytes accessed | tf_op | source)
XLA Modules:
  0.0 54.3 jit_solution(14925397230554738161)
XLA Ops:
  0.0 0.0 copy-start
  0.0 1.4 %copy-done = f32[2,3,16,32,128]{4,3,2,1,0:T(8,128)S(1)} copy-done((f32[2,3,16,32,128]{4,3,2,1,0:T(8,128)S(1)}, f32[2,3,16,32,128]{4,3,2,1,0:T(8,128)}, u32[]{:S(2)}) %copy-start) | copy-done | bytes 1572888
  1.4 0.0 copy-start.1
  1.4 0.9 %copy-done.1 = f32[16,32,128]{2,1,0:T(8,128)S(1)} copy-done((f32[16,32,128]{2,1,0:T(8,128)S(1)}, f32[16,32,128]{2,1,0:T(8,128)}, u32[]{:S(2)}) %copy-start.1) | copy-done | bytes 262168
  2.4 0.0 copy-start.2
  2.4 0.7 %copy-done.2 = f32[2]{0:T(128)S(1)} copy-done((f32[2]{0:T(128)S(1)}, f32[2]{0:T(128)}, u32[]{:S(2)}) %copy-start.2) | copy-done | bytes 32
  3.0 50.2 %shard_map.37 = (f32[2,16,32,128]{3,2,1,0:T(8,128)S(1)}, f32[2,128]{1,0:T(2,128)S(1)}) custom-call(f32[16,32,128]{2,1,0:T(8,128)S(1)} %copy-done.1, f32[6,16,32,128]{3,2,1,0:T(8,128)S(1)} %bitcast.1, f32[2]{0:T(128)S(1)} %copy-done.2), custom_call_target="tpu_custom_call" | custom-call | tf_op jit(solution)/shard_map/pallas_call | solution.py:523
  53.3 0.1 fusion
  53.4 0.9 %broadcast_multiply_fusion = f32[2,16,32,128]{3,2,1,0:T(8,128)} fusion(f32[2,16,32,128]{3,2,1,0:T(8,128)S(1)} %get-tuple-element.7, f32[2]{0:T(128)S(1)} %fusion), kind=kLoop, calls=%fused_computation | loop fusion | flops 131072 | bytes 1048584 | tf_op jit(solution)/shard_map/mul | solution.py:574
Async XLA Ops:
  0.0 1.4 %copy-start = (f32[2,3,16,32,128]{4,3,2,1,0:T(8,128)S(1)}, f32[2,3,16,32,128]{4,3,2,1,0:T(8,128)}, u32[]{:S(2)}) copy-start(f32[2,3,16,32,128]{4,3,2,1,0:T(8,128)} %param.4) | copy-start | bytes 4718596
  1.4 0.9 %copy-start.1 = (f32[16,32,128]{2,1,0:T(8,128)S(1)}, f32[16,32,128]{2,1,0:T(8,128)}, u32[]{:S(2)}) copy-start(f32[16,32,128]{2,1,0:T(8,128)} %refs_0_.1) | copy-start | bytes 786436
  2.4 0.7 %copy-start.2 = (f32[2]{0:T(128)S(1)}, f32[2]{0:T(128)}, u32[]{:S(2)}) copy-start(f32[2]{0:T(128)} %refs_2_.1) | copy-start | bytes 28

commit v2 on v1

v2 whole, which is shorter than its diff:
```python
import itertools
import math

import jax
import jax.numpy as jnp
from jax import lax
from jax.experimental import pallas as pl
from jax.experimental.pallas import tpu as pltpu
from jax.sharding import PartitionSpec as P

AXES = ("gx", "gy", "gz")
MESH = pl.DeviceIdType.MESH
TX, TY, TZ = 16, 32, 128
FLAT = [o for o in itertools.product((-1, 0, 1), (-1, 0, 1), (0,)) if o != (0, 0, 0)]
BELOW = [(0, 0, -1), (0, -1, -1), (-1, 0, -1), (-1, -1, -1)]
F32 = jnp.float32


def weight(i, j, k):
    return max(0.0, 3.0 - math.sqrt(i * i + j * j + k * k))


X_SPAN = {-1: (0, TX + 2, 2), 0: (0, 2, TX), 1: (TX - 2, 0, 2)}
Y_SPAN = {-1: (0, TY + 8, 2), 0: (0, 8, TY), 1: (TY - 2, 6, 2)}


def combine(values, weights):
    total = None
    for value, w in zip(values, weights):
        if w == 0.0:
            continue
        total = w * value if total is None else total + w * value
    return total


def loop(n, body, init, by=1):
    def block(q, carry):
        for i in range(by):
            carry = body(q * by + i, carry)
        return carry

    return block(0, init) if by == n else lax.fori_loop(0, n // by, block, init)


def kernel(
    sizes,
    design_ref,
    modes_ref,
    eig_ref,
    raw_ref,
    total_ref,
    dp,
    mb,
    mz,
    face,
    from_hi,
    wparts,
    fz,
    stiffs,
    mass_terms,
    gp,
    outs,
    z_out,
    z_up,
    z_down,
    a_in,
    b_in,
    eig,
    local_sem,
    out_sem,
    send_sem,
    recv_sem,
):
    cx, cy, cz = sizes
    me = tuple(lax.axis_index(a) for a in AXES)
    mx, my, mzi = me

    def near(o):
        return tuple(
            m if d == 0 else lax.rem(m + (d + s), s) for m, d, s in zip(me, o, sizes)
        )

    a_count, b_count = (cx // 2) * cz, 2 * cy
    a_slot = (mx // 2) * cz + mzi
    b_slot = lax.rem(mx, 2) * cy + my

    def a_device(k):
        slot = lax.rem(a_slot + k, a_count)
        return ((slot // cz) * 2 + lax.rem(mx, 2), my, lax.rem(slot, cz))

    def b_device(k):
        slot = lax.rem(b_slot + k, b_count)
        return ((mx // 2) * 2 + slot // cy, lax.rem(slot, cy), mzi)

    barrier = pltpu.get_barrier_semaphore()

    def greet(device):
        pl.semaphore_signal(barrier, inc=1, device_id=device, device_id_type=MESH)

    for o in FLAT + [(0, 0, 1)] + [tuple(-d for d in o) for o in BELOW[1:]] + [(0, 0, -1)]:
        greet(near(o))

    loads = [
        pltpu.make_async_copy(design_ref, dp.at[pl.ds(2, TX), pl.ds(8, TY)], local_sem.at[0])
    ]
    for c in range(6):
        loads.append(
            pltpu.make_async_copy(
                modes_ref.at[c], mb.at[c, pl.ds(0, TX), pl.ds(0, TY)], local_sem.at[1 + c]
            )
        )
    loads.append(pltpu.make_async_copy(eig_ref, eig, local_sem.at[7]))
    for load in loads:
        load.start()

    def greet_a(k, _):
        greet(a_device(k))
        return 0

    def greet_b(k, _):
        greet(b_device(k))
        return 0

    lax.fori_loop(1, a_count, greet_a, 0)
    lax.fori_loop(1, b_count, greet_b, 0)

    lane = lax.broadcasted_iota(jnp.int32, (8, 128), 1)
    quad = lax.shift_right_logical(lax.rem(lane + 2, 128), 2)
    first_two, last_two = lane < 2, lane >= 126
    zero = jnp.zeros((8, 128), F32)

    for load in loads:
        load.wait()

    def pack_modes(x, carry):
        carry = list(carry)
        for c in range(6):
            for g in range(4):
                k = (c % 2) * 64 + 4 * x + g
                r = pltpu.roll(mb[c, x, 8 * g : 8 * g + 8, :], k, 1)
                carry[c // 2] = jnp.where(lane == k, r, carry[c // 2])
        return tuple(carry)

    packed = loop(TX, pack_modes, (zero, zero, zero), TX)
    for i in range(3):
        face[i] = packed[i]

    pl.semaphore_wait(barrier, len(FLAT) + 2 + 3 + a_count - 1 + b_count - 1)

    sent = []

    def send(o, src, dst, sem):
        pltpu.make_async_remote_copy(
            src_ref=src,
            dst_ref=dst,
            send_sem=send_sem.at[sem],
            recv_sem=recv_sem.at[sem],
            device_id=near(o),
            device_id_type=MESH,
        ).start()

    def all_of(ref, sem):
        return pltpu.make_async_remote_copy(
            src_ref=ref,
            dst_ref=ref,
            send_sem=send_sem.at[sem],
            recv_sem=recv_sem.at[sem],
            device_id=near((0, 0, 1)),
            device_id_type=MESH,
        )

    for o in FLAT:
        (xs, xd, xn), (ys, yd, yn) = X_SPAN[o[0]], Y_SPAN[o[1]]
        send(
            o,
            design_ref.at[pl.ds(xs, xn), pl.ds(ys, yn)],
            dp.at[pl.ds(xd, xn), pl.ds(yd, yn)],
            0,
        )
    sent.append(all_of(dp.at[pl.ds(0, 13), pl.ds(0, 16)], 0))
    for o in ((-1, 0, 0), (0, -1, 0), (-1, -1, 0)):
        dx, dy, _ = o
        xs = pl.ds(0, 1) if dx else pl.ds(0, TX)
        xd = pl.ds(TX, 1) if dx else pl.ds(0, TX)
        ys = pl.ds(0, 1) if dy else pl.ds(0, TY)
        yd = pl.ds(TY, 1) if dy else pl.ds(0, TY)
        send(o, modes_ref.at[:, xs, ys], mb.at[:, xd, yd], 1)
    sent.append(all_of(mb.at[:, pl.ds(0, 7), pl.ds(0, 7)], 1))
    for o in BELOW:
        send(o, face, from_hi.at[-2 * o[0] - o[1]], 2)
    sent.append(all_of(from_hi, 2))

    def shift_modes(x, _):
        for c in range(6):
            for g in range(4):
                rows = slice(8 * g, 8 * g + 8)
                mz[c, x, rows, :] = pltpu.roll(mb[c, x, rows, :], 127, 1)
        return 0

    loop(TX, shift_modes, 0, 4)

    def inside(cell, total):
        return ((cell >= 0) & (cell < total)).astype(F32)

    zpos = mzi * TZ + lane
    z1 = inside(zpos - 1, cz * TZ) + inside(zpos + 1, cz * TZ)
    z2 = inside(zpos - 2, cz * TZ) + inside(zpos + 2, cz * TZ)
    for g in range(4):
        ypos = my * TY + 8 * g + lax.broadcasted_iota(jnp.int32, (8, 128), 0)
        y1 = inside(ypos - 1, cy * TY) + inside(ypos + 1, cy * TY)
        y2 = inside(ypos - 2, cy * TY) + inside(ypos + 2, cy * TY)
        for i in range(3):
            rows = [
                weight(i, j, 0) + weight(i, j, 1) * z1 + weight(i, j, 2) * z2 for j in range(3)
            ]
            wparts[i, g] = rows[0] + y1 * rows[1] + y2 * rows[2]

    y_hi = (my < cy - 1).astype(F32)
    x_hi = (mx < cx - 1).astype(F32)
    z_lo = (mzi > 0).astype(F32)
    z_hi = (mzi < cz - 1).astype(F32)

    def clear(ref, index, cond):
        @pl.when(cond)
        def _():
            ref[index] = jnp.zeros_like(ref[index])

    def clear_halo(ref, lead):
        clear(ref, lead + (slice(0, 2),), mx == 0)
        clear(ref, lead + (slice(TX + 2, TX + 4),), mx == cx - 1)
        clear(ref, lead + (slice(None), slice(0, 8)), my == 0)
        clear(ref, lead + (slice(None), slice(TY + 8, TY + 16)), my == cy - 1)

    order = ((0, 0), (0, 1), (1, 1), (0, 2), (1, 2), (2, 2))

    def sweep(load, put, packs):
        packs[0] = zero
        packs[1] = zero

        def body(xb, _):
            held = packs[xb // 2]
            for g in range(4):
                top = 8 + 8 * g
                a = {}
                for t in range(8):
                    p = 4 * xb + t
                    a[t, 0] = load(p, top, top + 8)
                    a[t, 1] = load(p, top - 1, top + 7) + load(p, top + 1, top + 9)
                    a[t, 2] = load(p, top - 2, top + 6) + load(p, top + 2, top + 10)
                for i in range(4):
                    b = {}
                    for j in range(3):
                        b[0, j] = a[i + 2, j]
                        b[1, j] = a[i + 1, j] + a[i + 3, j]
                        b[2, j] = a[i, j] + a[i + 4, j]
                    grouped = [b[u, v] if u == v else b[u, v] + b[v, u] for u, v in order]
                    e0, e1, e2 = (
                        combine(grouped, [weight(u, v, k) for u, v in order]) for k in range(3)
                    )
                    up, down = pltpu.roll(e1, 1, 1), pltpu.roll(e1, 127, 1)
                    up2, down2 = pltpu.roll(e2, 2, 1), pltpu.roll(e2, 126, 1)
                    out = jnp.where(lane < 1, up, jnp.where(lane >= 127, down, 0.0)) + jnp.where(
                        first_two, up2, jnp.where(last_two, down2, 0.0)
                    )
                    put(4 * xb + i, g, (e0 + ((up + down) + (up2 + down2))) - out)
                    k = lax.rem(xb, 2) * 16 + 4 * i + g
                    held = jnp.where(quad == k, pltpu.roll(out, 4 * k, 1), held)
            packs[xb // 2] = held
            return 0

        lax.fori_loop(0, 4, body, 0)

    def send_z(f):
        send((0, 0, -1), z_out.at[f], z_up.at[f], 3 + f)
        send((0, 0, 1), z_out.at[f], z_down.at[f], 6 + f)

    def merge_z(f):
        for s, ref in ((3 + f, z_up), (6 + f, z_down)):
            copy = all_of(ref.at[f], s)
            copy.wait_recv()
            sent.append(copy)
        for h in range(2):
            z_up[f, h] = jnp.where(lax.rem(lane, 4) >= 2, z_up[f, h] * z_hi, z_down[f, h] * z_lo)

    def from_z(f, xb, i, g):
        k = lax.rem(xb, 2) * 16 + 4 * i + g
        r = pltpu.roll(z_up[f, xb // 2], lax.rem(128 - 4 * k, 128), 1)
        return jnp.where(first_two | last_two, r, 0.0)

    sent[0].wait_recv()
    clear_halo(dp, ())

    def put_design(x, g, value):
        fz[x, 8 * g : 8 * g + 8, :] = value

    sweep(lambda p, a, b: dp[p, a:b, :], put_design, z_out.at[0])
    send_z(0)

    sent[1].wait_recv()
    sent[2].wait_recv()
    clear(mb, (slice(None), TX), mx == cx - 1)
    clear(mb, (slice(None), slice(None), slice(TY, TY + 8)), my == cy - 1)
    last = lane >= 127

    def patch_modes(x, _):
        for c in range(6):
            for g in range(5):
                k = (c % 2) * 64 + 4 * x + g % 4
                rows = slice(8 * g, 8 * g + 8)
                h = pltpu.roll(from_hi[g // 4, c // 2], lax.rem(255 - k, 128), 1)
                h = h * (z_hi * y_hi if g == 4 else z_hi)
                own = pltpu.roll(mb[c, x, rows, :], 127, 1) if g == 4 else mz[c, x, rows, :]
                mz[c, x, rows, :] = jnp.where(last, h, own)
        return 0

    loop(TX, patch_modes, 0, 2)

    def patch_end(c, _):
        for g in range(5):
            k = lax.rem(c, 2) * 64 + g % 4
            rows = slice(8 * g, 8 * g + 8)
            h = pltpu.roll(from_hi[2 + g // 4, c // 2], lax.rem(255 - k, 128), 1)
            h = h * (z_hi * x_hi * y_hi if g == 4 else z_hi * x_hi)
            mz[c, TX, rows, :] = jnp.where(last, h, pltpu.roll(mb[c, TX, rows, :], 127, 1))
        return 0

    loop(6, patch_end, 0, 3)

    factor = 1.0 / (1.3 * 0.4)
    lam, mu = 0.3 * factor, 0.2 * factor

    def plane(c, x, g):
        a, b = 8 * g, 8 * g + 8
        v0, v1 = mb[c, x, a:b, :], mb[c, x, a + 1 : b + 1, :]
        w0, w1 = mz[c, x, a:b, :], mz[c, x, a + 1 : b + 1, :]
        vs, vd, ws, wd = v0 + v1, v1 - v0, w0 + w1, w1 - w0
        return vs + ws, ws - vs, vd + wd, wd - vd

    def energies(now, later):
        a = {}
        for c in range(3):
            for q, (j, k) in enumerate(((0, 0), (0, 1), (1, 0), (1, 1))):
                a[c, 0, j, k] = now[4 * c + q] + later[4 * c + q]
                a[c, 1, j, k] = later[4 * c + q] - now[4 * c + q]
        s = {key: v * v for key, v in a.items()}

        def sq(v):
            return v * v

        q0 = s[0, 0, 0, 0] + s[1, 0, 0, 0] + s[2, 0, 0, 0]
        axial = s[0, 1, 0, 0] + s[1, 0, 1, 0] + s[2, 0, 0, 1]
        q1 = axial + (
            (s[0, 0, 1, 0] + s[0, 0, 0, 1])
            + (s[1, 1, 0, 0] + s[1, 0, 0, 1])
            + (s[2, 1, 0, 0] + s[2, 0, 1, 0])
        )
        bend = (
            (s[0, 1, 1, 0] + s[0, 1, 0, 1])
            + (s[1, 1, 1, 0] + s[1, 0, 1, 1])
            + (s[2, 1, 0, 1] + s[2, 0, 1, 1])
        )
        q2 = bend + (s[0, 0, 1, 1] + s[1, 1, 0, 1] + s[2, 1, 1, 0])
        q3 = s[0, 1, 1, 1] + s[1, 1, 1, 1] + s[2, 1, 1, 1]
        mass = (1 / 64) * q0 + (1 / 192) * q1 + ((1 / 576) * q2 + (1 / 1728) * q3)
        trace = sq(a[0, 1, 0, 0] + a[1, 0, 1, 0] + a[2, 0, 0, 1])
        shear = (
            sq(a[0, 0, 1, 0] + a[1, 1, 0, 0])
            + sq(a[1, 0, 0, 1] + a[2, 0, 1, 0])
            + sq(a[0, 0, 0, 1] + a[2, 1, 0, 0])
        )
        trace_1 = (
            sq(a[0, 1, 1, 0] + a[2, 0, 1, 1])
            + sq(a[0, 1, 0, 1] + a[1, 0, 1, 1])
            + sq(a[1, 1, 1, 0] + a[2, 1, 0, 1])
        )
        shear_1 = (
            sq(a[0, 0, 1, 1] + a[1, 1, 0, 1])
            + sq(a[1, 1, 0, 1] + a[2, 1, 1, 0])
            + sq(a[0, 0, 1, 1] + a[2, 1, 1, 0])
        )
        stiff = (
            ((lam / 16) * trace + (mu / 8) * axial)
            + ((mu / 16) * shear + (lam / 48) * trace_1)
            + ((mu / 16) * bend + (mu / 48) * shear_1)
            + ((lam + 4 * mu) / 144) * q3
        )
        return stiff, mass

    def element_pass(m, _):
        for pairs in range(2):
            groups = (2 * pairs, 2 * pairs + 1)

            def body(x, held):
                nexts = []
                for i, g in enumerate(groups):
                    later = sum((plane(3 * m + c, x + 1, g) for c in range(3)), ())
                    nexts += later
                    stiff, mass = energies(held[12 * i : 12 * i + 12], later)
                    stiffs[m, x, 8 * g : 8 * g + 8, :] = stiff
                    mass_terms[m, x, 8 * g : 8 * g + 8, :] = mass
                return tuple(nexts)

            first = []
            for g in groups:
                first += sum((plane(3 * m + c, 0, g) for c in range(3)), ())
            lax.fori_loop(0, TX, body, tuple(first))
        return 0

    lax.fori_loop(0, 2, element_pass, 0)

    top_t = math.tanh(4.0)
    merge_z(0)
    eigs = [eig[m] for m in range(2)]

    def project(xb, acc):
        acc = list(acc)
        for i in range(4):
            x = 4 * xb + i
            xpos = mx * TX + x
            x1 = inside(xpos - 1, cx * TX) + inside(xpos + 1, cx * TX)
            x2 = inside(xpos - 2, cx * TX) + inside(xpos + 2, cx * TX)
            for g in range(4):
                rows = slice(8 * g, 8 * g + 8)
                inverse = 1.0 / (wparts[0, g] + x1 * wparts[1, g] + x2 * wparts[2, g])
                t = jnp.tanh(8.0 * ((fz[x, rows, :] + from_z(0, xb, i, g)) * inverse - 0.5))
                rho = (top_t + t) * (0.5 / top_t)
                slope = (1.0 - t * t) * inverse * (4.0 / top_t)
                cubic = (3.0 * (1.0 - 0.001)) * (rho * rho)
                for m in range(2):
                    mass = mass_terms[m, x, rows, :]
                    acc[m] = acc[m] + rho * mass
                    gp[m, x + 2, 8 + 8 * g : 16 + 8 * g, :] = (
                        cubic * stiffs[m, x, rows, :] - eigs[m] * mass
                    ) * slope
        return tuple(acc)

    masses = lax.fori_loop(0, 4, project, (zero, zero))
    for m in range(2):
        a_in[0, m : m + 1, :] = jnp.sum(masses[m], axis=0, keepdims=True)

    for o in FLAT:
        (xs, xd, xn), (ys, yd, yn) = X_SPAN[o[0]], Y_SPAN[o[1]]
        send(
            o,
            gp.at[:, pl.ds(xs + 2, xn), pl.ds(ys + 8, yn)],
            gp.at[:, pl.ds(xd, xn), pl.ds(yd, yn)],
            9,
        )
    flats = all_of(gp.at[:, pl.ds(0, 13), pl.ds(0, 16)], 9)
    sent.append(flats)

    def spread_sum(ref, count, device, sem):
        def start(k, _):
            pltpu.make_async_remote_copy(
                src_ref=ref.at[0],
                dst_ref=ref.at[k],
                send_sem=send_sem.at[sem],
                recv_sem=recv_sem.at[sem],
                device_id=device(k),
                device_id_type=MESH,
            ).start()
            return 0

        lax.fori_loop(1, count, start, 0)
        copy = all_of(ref.at[pl.ds(1, count - 1)], sem)
        sent.append(copy)
        return copy

    a_copies = spread_sum(a_in, a_count, a_device, 10)

    flats.wait_recv()
    clear_halo(gp, (slice(None),))
    stores = []
    for m in range(2):

        def put_grad(x, g, value, m=m):
            outs[m, x, 8 * g : 8 * g + 8, :] = value

        sweep(lambda p, a, b, m=m: gp[m, p, a:b, :], put_grad, z_out.at[1 + m])
        send_z(1 + m)
        if m == 0:
            a_copies.wait_recv()
            b_in[0] = jnp.sum(a_in[...], axis=0)
            b_copies = spread_sum(b_in, b_count, b_device, 11)

    for m in range(2):
        merge_z(1 + m)

        def finish(xb, _, m=m):
            for i in range(4):
                for g in range(4):
                    rows = slice(8 * g, 8 * g + 8)
                    outs[m, 4 * xb + i, rows, :] = outs[m, 4 * xb + i, rows, :] + from_z(
                        1 + m, xb, i, g
                    )
            return 0

        lax.fori_loop(0, 4, finish, 0)
        store = pltpu.make_async_copy(outs.at[m], raw_ref.at[m], out_sem.at[m])
        store.start()
        stores.append(store)

    b_copies.wait_recv()
    total = jnp.sum(jnp.sum(b_in[...], axis=0), axis=1, keepdims=True)
    total_ref[...] = jnp.broadcast_to(total, (2, 128))

    for copies in sent:
        copies.wait_send()
    for store in stores:
        store.wait()


def per_device(sizes, design, modes, eigenvalues):
    cx, cy, cz = sizes
    a_count, b_count = (cx // 2) * cz, 2 * cy
    count = float(cx * TX * cy * TY * cz * TZ)
    dma = pltpu.SemaphoreType.DMA

    def vmem(*shape):
        return pltpu.VMEM(shape, F32)

    raw, total = pl.pallas_call(
        lambda *refs: kernel(sizes, *refs),
        out_shape=(
            jax.ShapeDtypeStruct((2, TX, TY, TZ), F32),
            jax.ShapeDtypeStruct((2, 128), F32),
        ),
        in_specs=[pl.BlockSpec(memory_space=pl.ANY)] * 3,
        out_specs=(
            pl.BlockSpec(memory_space=pl.ANY),
            pl.BlockSpec(memory_space=pltpu.VMEM),
        ),
        scratch_shapes=[
            vmem(TX + 4, TY + 16, TZ),
            vmem(6, TX + 1, TY + 8, TZ),
            vmem(6, TX + 1, TY + 8, TZ),
            vmem(3, 8, 128),
            vmem(4, 3, 8, 128),
            vmem(3, 4, 8, 128),
            vmem(TX, TY, TZ),
            vmem(2, TX, TY, TZ),
            vmem(2, TX, TY, TZ),
            vmem(2, TX + 4, TY + 16, TZ),
            vmem(2, TX, TY, TZ),
            vmem(3, 2, 8, 128),
            vmem(3, 2, 8, 128),
            vmem(3, 2, 8, 128),
            vmem(a_count, 2, 128),
            vmem(b_count, 2, 128),
            pltpu.SMEM((2,), F32),
            dma((8,)),
            dma((2,)),
            dma((12,)),
            dma((12,)),
        ],
        compiler_params=pltpu.CompilerParams(
            collective_id=0, has_side_effects=True, vmem_limit_bytes=62 * 1024 * 1024
        ),
    )(design, modes.reshape(6, TX, TY, TZ), eigenvalues)
    return raw * (count / total[:, 0])[:, None, None, None]


def solution(mesh):
    sizes = tuple(mesh.shape[a] for a in AXES)
    return jax.shard_map(
        lambda design, modes, eigenvalues: per_device(sizes, design, modes, eigenvalues),
        mesh=mesh,
        in_specs=(P("gx", "gy", "gz"), P(None, None, "gx", "gy", "gz"), P()),
        out_specs=P(None, "gx", "gy", "gz"),
        check_vma=False,
    )
```

time: 54.4 us -> 38.2 us (0.70)
  Pallas kernels: 50.2 us -> 35.3 us
  local copies, waits for them, and re-layouts: 3.01 us -> 0 us
  other arithmetic: 1.05 us -> 2.77 us
    pallas_call x1, Pallas kernels: 50.2 us -> 35.3 us  [per_device(): pl.pallas_call(lambda *refs: kernel(sizes, *refs), out_shape=(jax.ShapeDt...]
    unnamed x6 -> x0, local copies, waits for them, and re-layouts: 3.01 us -> none
    mul x1, other arithmetic: 0.93 us -> 1.97 us  [per_device(): return raw * (count / total[:, 0])[:, None, None, None]]
    div x1, other arithmetic: 0.12 us -> 0.8 us  [per_device(): return raw * (count / total[:, 0])[:, None, None, None]]
where the time goes in v2:
time: 38.2 us; the launch traced here: 38 us
  Pallas kernels  35.3 us (92%)
  other arithmetic  2.77 us (7%)
    pallas_call x1, Pallas kernels, per_device(): pl.pallas_call(lambda *refs: kernel(sizes, *refs), out_shape=(jax.ShapeDt...  35.3 us
    mul x1, other arithmetic, per_device(): return raw * (count / total[:, 0])[:, None, None, None]  1.97 us
    div x1, other arithmetic, per_device(): return raw * (count / total[:, 0])[:, None, None, None]  0.8 us

profile of v2, /device:TPU:1, one launch (start us, length us, event | category | flops | bytes accessed | tf_op | source)
XLA Modules:
  0.0 38.0 jit_solution(9786087918897519241)
XLA Ops:
  0.0 35.3 %shard_map.37 = (f32[2,16,32,128]{3,2,1,0:T(8,128)}, f32[2,128]{1,0:T(2,128)}) custom-call(f32[16,32,128]{2,1,0:T(8,128)} %refs_0_.1, f32[6,16,32,128]{3,2,1,0:T(8,128)} %bitcast.1, f32[2]{0:T(128)} %refs_2_.1), custom_call_target="tpu_custom_call" | custom-call | tf_op jit(solution)/shard_map/pallas_call | solution.py:522
  35.3 0.8 %fusion = f32[2]{0:T(128)S(1)} fusion(f32[2,128]{1,0:T(2,128)} %get-tuple-element.8), kind=kLoop, calls=%fused_computation.2 | loop fusion | flops 2 | bytes 16 | tf_op jit(solution)/shard_map/div | solution.py:560
  36.1 2.0 %broadcast_multiply_fusion = f32[2,16,32,128]{3,2,1,0:T(8,128)} fusion(f32[2,16,32,128]{3,2,1,0:T(8,128)} %get-tuple-element.7, f32[2]{0:T(128)S(1)} %fusion), kind=kLoop, calls=%fused_computation | loop fusion | flops 131072 | bytes 1048584 | tf_op jit(solution)/shard_map/mul | solution.py:560

commit v3 on v2

--- a/solution.py
+++ b/solution.py
@@ -76,20 +76,27 @@
     mx, my, mzi = me
 
     def near(o):
-        return tuple(
-            m if d == 0 else lax.rem(m + (d + s), s) for m, d, s in zip(me, o, sizes)
-        )
+        return tuple(m + d if d else m for m, d in zip(me, o))
+
+    def there(o):
+        ok = None
+        for m, d, size in zip(me, o, sizes):
+            if d:
+                here = m > 0 if d < 0 else m < size - 1
+                ok = here if ok is None else ok & here
+        return ok
+
+    def opposite(o):
+        return tuple(-d for d in o)
 
     a_count, b_count = (cx // 2) * cz, 2 * cy
     a_slot = (mx // 2) * cz + mzi
     b_slot = lax.rem(mx, 2) * cy + my
 
-    def a_device(k):
-        slot = lax.rem(a_slot + k, a_count)
+    def a_device(slot):
         return ((slot // cz) * 2 + lax.rem(mx, 2), my, lax.rem(slot, cz))
 
-    def b_device(k):
-        slot = lax.rem(b_slot + k, b_count)
+    def b_device(slot):
         return ((mx // 2) * 2 + slot // cy, lax.rem(slot, cy), mzi)
 
     barrier = pltpu.get_barrier_semaphore()
@@ -97,8 +104,14 @@
     def greet(device):
         pl.semaphore_signal(barrier, inc=1, device_id=device, device_id_type=MESH)
 
-    for o in FLAT + [(0, 0, 1)] + [tuple(-d for d in o) for o in BELOW[1:]] + [(0, 0, -1)]:
-        greet(near(o))
+    heard = a_count - 1 + b_count - 1
+    for o in FLAT + [(0, 0, 1), (0, 0, -1)] + BELOW[1:]:
+        heard = heard + there(o).astype(jnp.int32)
+    for o in FLAT + [(0, 0, 1), (0, 0, -1)] + [opposite(o) for o in BELOW[1:]]:
+
+        @pl.when(there(o))
+        def _(o=o):
+            greet(near(o))
 
     loads = [
         pltpu.make_async_copy(design_ref, dp.at[pl.ds(2, TX), pl.ds(8, TY)], local_sem.at[0])
@@ -114,11 +127,11 @@
         load.start()
 
     def greet_a(k, _):
-        greet(a_device(k))
+        greet(a_device(lax.rem(a_slot + k, a_count)))
         return 0
 
     def greet_b(k, _):
-        greet(b_device(k))
+        greet(b_device(lax.rem(b_slot + k, b_count)))
         return 0
 
     lax.fori_loop(1, a_count, greet_a, 0)
@@ -145,50 +158,63 @@
     for i in range(3):
         face[i] = packed[i]
 
-    pl.semaphore_wait(barrier, len(FLAT) + 2 + 3 + a_count - 1 + b_count - 1)
+    pl.semaphore_wait(barrier, heard)
 
     sent = []
 
-    def send(o, src, dst, sem):
-        pltpu.make_async_remote_copy(
+    def remote(src, dst, sem, device):
+        return pltpu.make_async_remote_copy(
             src_ref=src,
             dst_ref=dst,
             send_sem=send_sem.at[sem],
             recv_sem=recv_sem.at[sem],
-            device_id=near(o),
+            device_id=device,
             device_id_type=MESH,
-        ).start()
-
-    def all_of(ref, sem):
-        return pltpu.make_async_remote_copy(
-            src_ref=ref,
-            dst_ref=ref,
-            send_sem=send_sem.at[sem],
-            recv_sem=recv_sem.at[sem],
-            device_id=near((0, 0, 1)),
-            device_id_type=MESH,
-        )
-
-    for o in FLAT:
-        (xs, xd, xn), (ys, yd, yn) = X_SPAN[o[0]], Y_SPAN[o[1]]
-        send(
-            o,
-            design_ref.at[pl.ds(xs, xn), pl.ds(ys, yn)],
-            dp.at[pl.ds(xd, xn), pl.ds(yd, yn)],
-            0,
-        )
-    sent.append(all_of(dp.at[pl.ds(0, 13), pl.ds(0, 16)], 0))
-    for o in ((-1, 0, 0), (0, -1, 0), (-1, -1, 0)):
+        )
+
+    def send(o, src, dst, sem):
+        @pl.when(there(o))
+        def _():
+            remote(src, dst, sem, near(o)).start()
+
+        def sent_all():
+            @pl.when(there(o))
+            def _():
+                remote(src, dst, sem, near(o)).wait_send()
+
+        def received():
+            @pl.when(there(opposite(o)))
+            def _():
+                remote(src, dst, sem, near(o)).wait_recv()
+
+        sent.append(sent_all)
+        return received
+
+    def send_flats(src, dst, lead, shift, sem):
+        waits = []
+        for i, o in enumerate(FLAT):
+            (xs, xd, xn), (ys, yd, yn) = X_SPAN[o[0]], Y_SPAN[o[1]]
+            waits.append(
+                send(
+                    o,
+                    src.at[lead + (pl.ds(xs + shift[0], xn), pl.ds(ys + shift[1], yn))],
+                    dst.at[lead + (pl.ds(xd, xn), pl.ds(yd, yn))],
+                    sem + i,
+                )
+            )
+        return waits
+
+    design_waits = send_flats(design_ref, dp, (), (0, 0), 0)
+    mode_waits = []
+    for i, o in enumerate(((-1, 0, 0), (0, -1, 0), (-1, -1, 0))):
         dx, dy, _ = o
         xs = pl.ds(0, 1) if dx else pl.ds(0, TX)
         xd = pl.ds(TX, 1) if dx else pl.ds(0, TX)
         ys = pl.ds(0, 1) if dy else pl.ds(0, TY)
         yd = pl.ds(TY, 1) if dy else pl.ds(0, TY)
-        send(o, modes_ref.at[:, xs, ys], mb.at[:, xd, yd], 1)
-    sent.append(all_of(mb.at[:, pl.ds(0, 7), pl.ds(0, 7)], 1))
-    for o in BELOW:
-        send(o, face, from_hi.at[-2 * o[0] - o[1]], 2)
-    sent.append(all_of(from_hi, 2))
+        mode_waits.append(send(o, modes_ref.at[:, xs, ys], mb.at[:, xd, yd], 8 + i))
+    for i, o in enumerate(BELOW):
+        mode_waits.append(send(o, face, from_hi.at[-2 * o[0] - o[1]], 11 + i))
 
     def shift_modes(x, _):
         for c in range(6):
@@ -214,11 +240,6 @@
                 weight(i, j, 0) + weight(i, j, 1) * z1 + weight(i, j, 2) * z2 for j in range(3)
             ]
             wparts[i, g] = rows[0] + y1 * rows[1] + y2 * rows[2]
-
-    y_hi = (my < cy - 1).astype(F32)
-    x_hi = (mx < cx - 1).astype(F32)
-    z_lo = (mzi > 0).astype(F32)
-    z_hi = (mzi < cz - 1).astype(F32)
 
     def clear(ref, index, cond):
         @pl.when(cond)
@@ -271,33 +292,38 @@
         lax.fori_loop(0, 4, body, 0)
 
     def send_z(f):
-        send((0, 0, -1), z_out.at[f], z_up.at[f], 3 + f)
-        send((0, 0, 1), z_out.at[f], z_down.at[f], 6 + f)
-
-    def merge_z(f):
-        for s, ref in ((3 + f, z_up), (6 + f, z_down)):
-            copy = all_of(ref.at[f], s)
-            copy.wait_recv()
-            sent.append(copy)
+        return (
+            send((0, 0, -1), z_out.at[f], z_up.at[f], 23 + f),
+            send((0, 0, 1), z_out.at[f], z_down.at[f], 26 + f),
+        )
+
+    def merge_z(f, waits):
+        for wait in waits:
+            wait()
+        clear(z_up, f, mzi == cz - 1)
+        clear(z_down, f, mzi == 0)
         for h in range(2):
-            z_up[f, h] = jnp.where(lax.rem(lane, 4) >= 2, z_up[f, h] * z_hi, z_down[f, h] * z_lo)
+            z_up[f, h] = jnp.where(lax.rem(lane, 4) >= 2, z_up[f, h], z_down[f, h])
 
     def from_z(f, xb, i, g):
         k = lax.rem(xb, 2) * 16 + 4 * i + g
         r = pltpu.roll(z_up[f, xb // 2], lax.rem(128 - 4 * k, 128), 1)
         return jnp.where(first_two | last_two, r, 0.0)
 
-    sent[0].wait_recv()
+    for wait in design_waits:
+        wait()
     clear_halo(dp, ())
 
     def put_design(x, g, value):
         fz[x, 8 * g : 8 * g + 8, :] = value
 
     sweep(lambda p, a, b: dp[p, a:b, :], put_design, z_out.at[0])
-    send_z(0)
-
-    sent[1].wait_recv()
-    sent[2].wait_recv()
+    z_waits = [send_z(0)]
+
+    for wait in mode_waits:
+        wait()
+    for o in BELOW:
+        clear(from_hi, -2 * o[0] - o[1], jnp.logical_not(there(opposite(o))))
     clear(mb, (slice(None), TX), mx == cx - 1)
     clear(mb, (slice(None), slice(None), slice(TY, TY + 8)), my == cy - 1)
     last = lane >= 127
@@ -308,7 +334,6 @@
                 k = (c % 2) * 64 + 4 * x + g % 4
                 rows = slice(8 * g, 8 * g + 8)
                 h = pltpu.roll(from_hi[g // 4, c // 2], lax.rem(255 - k, 128), 1)
-                h = h * (z_hi * y_hi if g == 4 else z_hi)
                 own = pltpu.roll(mb[c, x, rows, :], 127, 1) if g == 4 else mz[c, x, rows, :]
                 mz[c, x, rows, :] = jnp.where(last, h, own)
         return 0
@@ -320,7 +345,6 @@
             k = lax.rem(c, 2) * 64 + g % 4
             rows = slice(8 * g, 8 * g + 8)
             h = pltpu.roll(from_hi[2 + g // 4, c // 2], lax.rem(255 - k, 128), 1)
-            h = h * (z_hi * x_hi * y_hi if g == 4 else z_hi * x_hi)
             mz[c, TX, rows, :] = jnp.where(last, h, pltpu.roll(mb[c, TX, rows, :], 127, 1))
         return 0
 
@@ -409,7 +433,7 @@
     lax.fori_loop(0, 2, element_pass, 0)
 
     top_t = math.tanh(4.0)
-    merge_z(0)
+    merge_z(0, z_waits[0])
     eigs = [eig[m] for m in range(2)]
 
     def project(xb, acc):
@@ -436,39 +460,24 @@
 
     masses = lax.fori_loop(0, 4, project, (zero, zero))
     for m in range(2):
-        a_in[0, m : m + 1, :] = jnp.sum(masses[m], axis=0, keepdims=True)
-
-    for o in FLAT:
-        (xs, xd, xn), (ys, yd, yn) = X_SPAN[o[0]], Y_SPAN[o[1]]
-        send(
-            o,
-            gp.at[:, pl.ds(xs + 2, xn), pl.ds(ys + 8, yn)],
-            gp.at[:, pl.ds(xd, xn), pl.ds(yd, yn)],
-            9,
-        )
-    flats = all_of(gp.at[:, pl.ds(0, 13), pl.ds(0, 16)], 9)
-    sent.append(flats)
-
-    def spread_sum(ref, count, device, sem):
+        a_in[a_slot, m : m + 1, :] = jnp.sum(masses[m], axis=0, keepdims=True)
+
+    def spread_sum(ref, count, slot, device, sem):
         def start(k, _):
-            pltpu.make_async_remote_copy(
-                src_ref=ref.at[0],
-                dst_ref=ref.at[k],
-                send_sem=send_sem.at[sem],
-                recv_sem=recv_sem.at[sem],
-                device_id=device(k),
-                device_id_type=MESH,
-            ).start()
+            @pl.when(k != slot)
+            def _():
+                remote(ref.at[slot], ref.at[slot], sem, device(k)).start()
+
             return 0
 
-        lax.fori_loop(1, count, start, 0)
-        copy = all_of(ref.at[pl.ds(1, count - 1)], sem)
-        sent.append(copy)
-        return copy
-
-    a_copies = spread_sum(a_in, a_count, a_device, 10)
-
-    flats.wait_recv()
+        lax.fori_loop(0, count, start, 0)
+        return remote(ref.at[pl.ds(0, count - 1)], ref.at[pl.ds(0, count - 1)], sem, me)
+
+    a_copies = spread_sum(a_in, a_count, a_slot, a_device, 29)
+    flats = send_flats(gp, gp, (slice(None),), (2, 8), 15)
+
+    for wait in flats:
+        wait()
     clear_halo(gp, (slice(None),))
     stores = []
     for m in range(2):
@@ -477,14 +486,14 @@
             outs[m, x, 8 * g : 8 * g + 8, :] = value
 
         sweep(lambda p, a, b, m=m: gp[m, p, a:b, :], put_grad, z_out.at[1 + m])
-        send_z(1 + m)
-        if m == 0:
-            a_copies.wait_recv()
-            b_in[0] = jnp.sum(a_in[...], axis=0)
-            b_copies = spread_sum(b_in, b_count, b_device, 11)
+        z_waits.append(send_z(1 + m))
+
+    a_copies.wait_recv()
+    b_in[b_slot] = jnp.sum(a_in[...], axis=0)
+    b_copies = spread_sum(b_in, b_count, b_slot, b_device, 30)
 
     for m in range(2):
-        merge_z(1 + m)
+        merge_z(1 + m, z_waits[1 + m])
 
         def finish(xb, _, m=m):
             for i in range(4):
@@ -504,8 +513,10 @@
     total = jnp.sum(jnp.sum(b_in[...], axis=0), axis=1, keepdims=True)
     total_ref[...] = jnp.broadcast_to(total, (2, 128))
 
-    for copies in sent:
-        copies.wait_send()
+    for wait in sent:
+        wait()
+    a_copies.wait_send()
+    b_copies.wait_send()
     for store in stores:
         store.wait()
 
@@ -550,8 +561,8 @@
             pltpu.SMEM((2,), F32),
             dma((8,)),
             dma((2,)),
-            dma((12,)),
-            dma((12,)),
+            dma((31,)),
+            dma((31,)),
         ],
         compiler_params=pltpu.CompilerParams(
             collective_id=0, has_side_effects=True, vmem_limit_bytes=62 * 1024 * 1024

time: 38.2 us -> 35.5 us (0.929)
  Pallas kernels: 35.3 us -> 32.5 us
    pallas_call x1, Pallas kernels: 35.3 us -> 32.5 us  [per_device(): pl.pallas_call(lambda *refs: kernel(sizes, *refs), out_shape=(jax.ShapeDt...]
where the time goes in v3:
time: 35.5 us; the launch traced here: 35.3 us
  Pallas kernels  32.5 us (92%)
  other arithmetic  2.77 us (8%)
    pallas_call x1, Pallas kernels, per_device(): pl.pallas_call(lambda *refs: kernel(sizes, *refs), out_shape=(jax.ShapeDt...  32.5 us
    mul x1, other arithmetic, per_device(): return raw * (count / total[:, 0])[:, None, None, None]  1.97 us
    div x1, other arithmetic, per_device(): return raw * (count / total[:, 0])[:, None, None, None]  0.8 us

profile of v3, /device:TPU:1, one launch (start us, length us, event | category | flops | bytes accessed | tf_op | source)
XLA Modules:
  0.0 35.3 jit_solution(6876282929420484873)
XLA Ops:
  0.0 32.5 %shard_map.37 = (f32[2,16,32,128]{3,2,1,0:T(8,128)}, f32[2,128]{1,0:T(2,128)}) custom-call(f32[16,32,128]{2,1,0:T(8,128)} %refs_0_.1, f32[6,16,32,128]{3,2,1,0:T(8,128)} %bitcast.1, f32[2]{0:T(128)} %refs_2_.1), custom_call_target="tpu_custom_call" | custom-call | tf_op jit(solution)/shard_map/pallas_call | solution.py:533
  32.5 0.8 %fusion = f32[2]{0:T(128)S(1)} fusion(f32[2,128]{1,0:T(2,128)} %get-tuple-element.8), kind=kLoop, calls=%fused_computation.2 | loop fusion | flops 2 | bytes 16 | tf_op jit(solution)/shard_map/div | solution.py:571
  33.3 2.0 %broadcast_multiply_fusion = f32[2,16,32,128]{3,2,1,0:T(8,128)} fusion(f32[2,16,32,128]{3,2,1,0:T(8,128)} %get-tuple-element.7, f32[2]{0:T(128)S(1)} %fusion), kind=kLoop, calls=%fused_computation | loop fusion | flops 131072 | bytes 1048584 | tf_op jit(solution)/shard_map/mul | solution.py:571

commit v4 on v3

--- a/solution.py
+++ b/solution.py
@@ -12,6 +12,7 @@
 MESH = pl.DeviceIdType.MESH
 TX, TY, TZ = 16, 32, 128
 FLAT = [o for o in itertools.product((-1, 0, 1), (-1, 0, 1), (0,)) if o != (0, 0, 0)]
+SIDES = [(-1, 0, 0), (0, -1, 0), (-1, -1, 0)]
 BELOW = [(0, 0, -1), (0, -1, -1), (-1, 0, -1), (-1, -1, -1)]
 F32 = jnp.float32
 
@@ -48,12 +49,14 @@
     modes_ref,
     eig_ref,
     raw_ref,
-    total_ref,
+    scale_ref,
     dp,
     mb,
     mz,
     face,
     from_hi,
+    from_side,
+    edge,
     wparts,
     fz,
     stiffs,
@@ -72,6 +75,7 @@
     recv_sem,
 ):
     cx, cy, cz = sizes
+    count = float(cx * TX * cy * TY * cz * TZ)
     me = tuple(lax.axis_index(a) for a in AXES)
     mx, my, mzi = me
 
@@ -141,22 +145,6 @@
     quad = lax.shift_right_logical(lax.rem(lane + 2, 128), 2)
     first_two, last_two = lane < 2, lane >= 126
     zero = jnp.zeros((8, 128), F32)
-
-    for load in loads:
-        load.wait()
-
-    def pack_modes(x, carry):
-        carry = list(carry)
-        for c in range(6):
-            for g in range(4):
-                k = (c % 2) * 64 + 4 * x + g
-                r = pltpu.roll(mb[c, x, 8 * g : 8 * g + 8, :], k, 1)
-                carry[c // 2] = jnp.where(lane == k, r, carry[c // 2])
-        return tuple(carry)
-
-    packed = loop(TX, pack_modes, (zero, zero, zero), TX)
-    for i in range(3):
-        face[i] = packed[i]
 
     pl.semaphore_wait(barrier, heard)
 
@@ -206,15 +194,37 @@
 
     design_waits = send_flats(design_ref, dp, (), (0, 0), 0)
     mode_waits = []
-    for i, o in enumerate(((-1, 0, 0), (0, -1, 0), (-1, -1, 0))):
+    for i, o in enumerate(SIDES):
         dx, dy, _ = o
         xs = pl.ds(0, 1) if dx else pl.ds(0, TX)
         xd = pl.ds(TX, 1) if dx else pl.ds(0, TX)
         ys = pl.ds(0, 1) if dy else pl.ds(0, TY)
         yd = pl.ds(TY, 1) if dy else pl.ds(0, TY)
         mode_waits.append(send(o, modes_ref.at[:, xs, ys], mb.at[:, xd, yd], 8 + i))
+
+    for load in loads:
+        load.wait()
+
+    def pack_modes(x, carry):
+        first, final = (list(v) for v in carry)
+        for c in range(6):
+            for g in range(4):
+                k = (c // 3) * 64 + 4 * x + g
+                r = pltpu.roll(mb[c, x, 8 * g : 8 * g + 8, :], k, 1)
+                first[c % 3] = jnp.where(lane == k, r, first[c % 3])
+                final[c % 3] = jnp.where(lane == (k + 127) % 128, r, final[c % 3])
+        return tuple(first), tuple(final)
+
+    first, final = loop(TX, pack_modes, ((zero,) * 3, (zero,) * 3), TX)
+    for c in range(3):
+        face[0, c] = first[c]
+        face[1, c] = pltpu.roll(final[c], 1, 1)
+
+    face_waits = []
     for i, o in enumerate(BELOW):
-        mode_waits.append(send(o, face, from_hi.at[-2 * o[0] - o[1]], 11 + i))
+        face_waits.append(send(o, face.at[0], from_hi.at[-2 * o[0] - o[1]], 11 + i))
+    for i, o in enumerate(SIDES):
+        face_waits.append(send(o, face.at[1], from_side.at[-2 * o[0] - o[1]], 31 + i))
 
     def shift_modes(x, _):
         for c in range(6):
@@ -322,43 +332,30 @@
 
     for wait in mode_waits:
         wait()
-    for o in BELOW:
-        clear(from_hi, -2 * o[0] - o[1], jnp.logical_not(there(opposite(o))))
     clear(mb, (slice(None), TX), mx == cx - 1)
     clear(mb, (slice(None), slice(None), slice(TY, TY + 8)), my == cy - 1)
-    last = lane >= 127
-
-    def patch_modes(x, _):
-        for c in range(6):
-            for g in range(5):
-                k = (c % 2) * 64 + 4 * x + g % 4
-                rows = slice(8 * g, 8 * g + 8)
-                h = pltpu.roll(from_hi[g // 4, c // 2], lax.rem(255 - k, 128), 1)
-                own = pltpu.roll(mb[c, x, rows, :], 127, 1) if g == 4 else mz[c, x, rows, :]
-                mz[c, x, rows, :] = jnp.where(last, h, own)
+
+    def shift_halo(c, _):
+        for x in range(TX + 1):
+            mz[c, x, TY : TY + 8, :] = pltpu.roll(mb[c, x, TY : TY + 8, :], 127, 1)
+        for g in range(4):
+            rows = slice(8 * g, 8 * g + 8)
+            mz[c, TX, rows, :] = pltpu.roll(mb[c, TX, rows, :], 127, 1)
         return 0
 
-    loop(TX, patch_modes, 0, 2)
-
-    def patch_end(c, _):
-        for g in range(5):
-            k = lax.rem(c, 2) * 64 + g % 4
-            rows = slice(8 * g, 8 * g + 8)
-            h = pltpu.roll(from_hi[2 + g // 4, c // 2], lax.rem(255 - k, 128), 1)
-            mz[c, TX, rows, :] = jnp.where(last, h, pltpu.roll(mb[c, TX, rows, :], 127, 1))
-        return 0
-
-    loop(6, patch_end, 0, 3)
+    loop(6, shift_halo, 0, 2)
 
     factor = 1.0 / (1.3 * 0.4)
     lam, mu = 0.3 * factor, 0.2 * factor
+
+    def across(v0, v1, w0, w1):
+        vs, vd, ws, wd = v0 + v1, v1 - v0, w0 + w1, w1 - w0
+        return vs + ws, ws - vs, vd + wd, wd - vd
 
     def plane(c, x, g):
         a, b = 8 * g, 8 * g + 8
         v0, v1 = mb[c, x, a:b, :], mb[c, x, a + 1 : b + 1, :]
-        w0, w1 = mz[c, x, a:b, :], mz[c, x, a + 1 : b + 1, :]
-        vs, vd, ws, wd = v0 + v1, v1 - v0, w0 + w1, w1 - w0
-        return vs + ws, ws - vs, vd + wd, wd - vd
+        return across(v0, v1, mz[c, x, a:b, :], mz[c, x, a + 1 : b + 1, :])
 
     def energies(now, later):
         a = {}
@@ -431,6 +428,36 @@
         return 0
 
     lax.fori_loop(0, 2, element_pass, 0)
+
+    for wait in face_waits:
+        wait()
+    for o in BELOW:
+        clear(from_hi, -2 * o[0] - o[1], jnp.logical_not(there(opposite(o))))
+    for o in SIDES:
+        clear(from_side, -2 * o[0] - o[1], jnp.logical_not(there(opposite(o))))
+    below_last = lax.broadcasted_iota(jnp.int32, (8, 128), 0) < 7
+    last_group, last_plane = lax.rem(lane, 4) == 3, lax.rem(lane, 64) >= 60
+
+    def next_y(own, halo):
+        own, halo = pltpu.roll(own, 7, 0), pltpu.roll(halo, 7, 0)
+        over = jnp.where(last_group, pltpu.roll(halo, 3, 1), pltpu.roll(own, 127, 1))
+        return jnp.where(below_last, own, over)
+
+    def next_x(own, halo):
+        return jnp.where(last_plane, pltpu.roll(halo, 60, 1), pltpu.roll(own, 124, 1))
+
+    now, later = (), ()
+    for c in range(3):
+        sides = []
+        for own, side in ((face[1, c], from_side), (from_hi[0, c], from_hi)):
+            own_y, x_halo = next_y(own, side[1, c]), side[2, c]
+            x_halo_y = next_y(x_halo, side[3, c])
+            sides.append((own, own_y, next_x(own, x_halo), next_x(own_y, x_halo_y)))
+        (v00, v01, v10, v11), (w00, w01, w10, w11) = sides
+        now += across(v00, v01, w00, w01)
+        later += across(v10, v11, w10, w11)
+    edge[0], edge[1] = energies(now, later)
+    last = lane >= 127
 
     top_t = math.tanh(4.0)
     merge_z(0, z_waits[0])
@@ -451,10 +478,12 @@
                 slope = (1.0 - t * t) * inverse * (4.0 / top_t)
                 cubic = (3.0 * (1.0 - 0.001)) * (rho * rho)
                 for m in range(2):
-                    mass = mass_terms[m, x, rows, :]
+                    turn = lax.rem(255 - (64 * m + 4 * x + g), 128)
+                    mass = jnp.where(last, pltpu.roll(edge[1], turn, 1), mass_terms[m, x, rows, :])
+                    stiff = jnp.where(last, pltpu.roll(edge[0], turn, 1), stiffs[m, x, rows, :])
                     acc[m] = acc[m] + rho * mass
                     gp[m, x + 2, 8 + 8 * g : 16 + 8 * g, :] = (
-                        cubic * stiffs[m, x, rows, :] - eigs[m] * mass
+                        cubic * stiff - eigs[m] * mass
                     ) * slope
         return tuple(acc)
 
@@ -511,7 +540,7 @@
 
     b_copies.wait_recv()
     total = jnp.sum(jnp.sum(b_in[...], axis=0), axis=1, keepdims=True)
-    total_ref[...] = jnp.broadcast_to(total, (2, 128))
+    scale_ref[...] = jnp.broadcast_to(count / total, (2, 128))
 
     for wait in sent:
         wait()
@@ -524,13 +553,12 @@
 def per_device(sizes, design, modes, eigenvalues):
     cx, cy, cz = sizes
     a_count, b_count = (cx // 2) * cz, 2 * cy
-    count = float(cx * TX * cy * TY * cz * TZ)
     dma = pltpu.SemaphoreType.DMA
 
     def vmem(*shape):
         return pltpu.VMEM(shape, F32)
 
-    raw, total = pl.pallas_call(
+    raw, scale = pl.pallas_call(
         lambda *refs: kernel(sizes, *refs),
         out_shape=(
             jax.ShapeDtypeStruct((2, TX, TY, TZ), F32),
@@ -545,8 +573,10 @@
             vmem(TX + 4, TY + 16, TZ),
             vmem(6, TX + 1, TY + 8, TZ),
             vmem(6, TX + 1, TY + 8, TZ),
-            vmem(3, 8, 128),
+            vmem(2, 3, 8, 128),
             vmem(4, 3, 8, 128),
+            vmem(4, 3, 8, 128),
+            vmem(2, 8, 128),
             vmem(3, 4, 8, 128),
             vmem(TX, TY, TZ),
             vmem(2, TX, TY, TZ),
@@ -561,14 +591,14 @@
             pltpu.SMEM((2,), F32),
             dma((8,)),
             dma((2,)),
-            dma((31,)),
-            dma((31,)),
+            dma((34,)),
+            dma((34,)),
         ],
         compiler_params=pltpu.CompilerParams(
             collective_id=0, has_side_effects=True, vmem_limit_bytes=62 * 1024 * 1024
         ),
     )(design, modes.reshape(6, TX, TY, TZ), eigenvalues)
-    return raw * (count / total[:, 0])[:, None, None, None]
+    return raw * scale[:, :1, None, None]
 
 
 def solution(mesh):

time: 35.5 us -> 34.4 us (0.969)
  Pallas kernels: 32.5 us -> 31.5 us
  other arithmetic: 2.77 us -> 1.96 us
  local copies, waits for them, and re-layouts: 0 us -> 0.8 us
    pallas_call x1, Pallas kernels: 32.5 us -> 31.5 us  [per_device(): pl.pallas_call(lambda *refs: kernel(sizes, *refs), out_shape=(jax.ShapeDt...]
    div x1 -> x0, other arithmetic: 0.8 us -> none  [per_device(): return raw * (count / total[:, 0])[:, None, None, None]]
    slice x0 -> x1, local copies, waits for them, and re-layouts: none -> 0.8 us  [per_device(): return raw * scale[:, :1, None, None]]
where the time goes in v4:
time: 34.4 us; the launch traced here: 34.3 us
  Pallas kernels  31.5 us (92%)
  other arithmetic  1.96 us (6%)
  local copies, waits for them, and re-layouts  0.8 us (2%)
    pallas_call x1, Pallas kernels, per_device(): pl.pallas_call(lambda *refs: kernel(sizes, *refs), out_shape=(jax.ShapeDt...  31.5 us
    mul x1, other arithmetic, per_device(): return raw * scale[:, :1, None, None]  1.96 us
    slice x1, local copies, waits for them, and re-layouts, per_device(): return raw * scale[:, :1, None, None]  0.8 us

profile of v4, /device:TPU:1, one launch (start us, length us, event | category | flops | bytes accessed | tf_op | source)
XLA Modules:
  0.0 34.3 jit_solution(16560321690271437476)
XLA Ops:
  0.0 31.5 %shard_map.37 = (f32[2,16,32,128]{3,2,1,0:T(8,128)}, f32[2,128]{1,0:T(2,128)}) custom-call(f32[16,32,128]{2,1,0:T(8,128)} %refs_0_.1, f32[6,16,32,128]{3,2,1,0:T(8,128)} %bitcast.1, f32[2]{0:T(128)} %refs_2_.1), custom_call_target="tpu_custom_call" | custom-call | tf_op jit(solution)/shard_map/pallas_call | solution.py:561
  31.5 0.8 %slice_reduce_fusion = f32[2]{0:T(128)S(1)} fusion(f32[2,128]{1,0:T(2,128)} %get-tuple-element.8), kind=kLoop, calls=%fused_computation.1 | loop fusion | bytes 16 | tf_op jit(solution)/shard_map/slice | solution.py:601
  32.3 2.0 %broadcast_multiply_fusion = f32[2,16,32,128]{3,2,1,0:T(8,128)} fusion(f32[2,16,32,128]{3,2,1,0:T(8,128)} %get-tuple-element.7, f32[2]{0:T(128)S(1)} %slice_reduce_fusion), kind=kLoop, calls=%fused_computation | loop fusion | flops 131072 | bytes 1048584 | tf_op jit(solution)/shard_map/mul | solution.py:601

commit v5 on v4

--- a/solution.py
+++ b/solution.py
@@ -1,3 +1,4 @@
+import functools
 import itertools
 import math
 
@@ -108,6 +109,17 @@
     def greet(device):
         pl.semaphore_signal(barrier, inc=1, device_id=device, device_id_type=MESH)
 
+    def greet_a(k, _):
+        greet(a_device(lax.rem(a_slot + k, a_count)))
+        return 0
+
+    def greet_b(k, _):
+        greet(b_device(lax.rem(b_slot + k, b_count)))
+        return 0
+
+    lax.fori_loop(1, a_count, greet_a, 0)
+    lax.fori_loop(1, b_count, greet_b, 0)
+
     heard = a_count - 1 + b_count - 1
     for o in FLAT + [(0, 0, 1), (0, 0, -1)] + BELOW[1:]:
         heard = heard + there(o).astype(jnp.int32)
@@ -129,17 +141,6 @@
     loads.append(pltpu.make_async_copy(eig_ref, eig, local_sem.at[7]))
     for load in loads:
         load.start()
-
-    def greet_a(k, _):
-        greet(a_device(lax.rem(a_slot + k, a_count)))
-        return 0
-
-    def greet_b(k, _):
-        greet(b_device(lax.rem(b_slot + k, b_count)))
-        return 0
-
-    lax.fori_loop(1, a_count, greet_a, 0)
-    lax.fori_loop(1, b_count, greet_b, 0)
 
     lane = lax.broadcasted_iota(jnp.int32, (8, 128), 1)
     quad = lax.shift_right_logical(lax.rem(lane + 2, 128), 2)
@@ -192,7 +193,8 @@
             )
         return waits
 
-    design_waits = send_flats(design_ref, dp, (), (0, 0), 0)
+    loads[0].wait()
+    design_waits = send_flats(dp, dp, (), (2, 8), 0)
     mode_waits = []
     for i, o in enumerate(SIDES):
         dx, dy, _ = o
@@ -201,39 +203,6 @@
         ys = pl.ds(0, 1) if dy else pl.ds(0, TY)
         yd = pl.ds(TY, 1) if dy else pl.ds(0, TY)
         mode_waits.append(send(o, modes_ref.at[:, xs, ys], mb.at[:, xd, yd], 8 + i))
-
-    for load in loads:
-        load.wait()
-
-    def pack_modes(x, carry):
-        first, final = (list(v) for v in carry)
-        for c in range(6):
-            for g in range(4):
-                k = (c // 3) * 64 + 4 * x + g
-                r = pltpu.roll(mb[c, x, 8 * g : 8 * g + 8, :], k, 1)
-                first[c % 3] = jnp.where(lane == k, r, first[c % 3])
-                final[c % 3] = jnp.where(lane == (k + 127) % 128, r, final[c % 3])
-        return tuple(first), tuple(final)
-
-    first, final = loop(TX, pack_modes, ((zero,) * 3, (zero,) * 3), TX)
-    for c in range(3):
-        face[0, c] = first[c]
-        face[1, c] = pltpu.roll(final[c], 1, 1)
-
-    face_waits = []
-    for i, o in enumerate(BELOW):
-        face_waits.append(send(o, face.at[0], from_hi.at[-2 * o[0] - o[1]], 11 + i))
-    for i, o in enumerate(SIDES):
-        face_waits.append(send(o, face.at[1], from_side.at[-2 * o[0] - o[1]], 31 + i))
-
-    def shift_modes(x, _):
-        for c in range(6):
-            for g in range(4):
-                rows = slice(8 * g, 8 * g + 8)
-                mz[c, x, rows, :] = pltpu.roll(mb[c, x, rows, :], 127, 1)
-        return 0
-
-    loop(TX, shift_modes, 0, 4)
 
     def inside(cell, total):
         return ((cell >= 0) & (cell < total)).astype(F32)
@@ -250,6 +219,39 @@
                 weight(i, j, 0) + weight(i, j, 1) * z1 + weight(i, j, 2) * z2 for j in range(3)
             ]
             wparts[i, g] = rows[0] + y1 * rows[1] + y2 * rows[2]
+
+    for load in loads[1:]:
+        load.wait()
+
+    def pack_modes(x, carry):
+        first, final = (list(v) for v in carry)
+        for c in range(6):
+            for g in range(4):
+                k = (c // 3) * 64 + 4 * x + g
+                r = pltpu.roll(mb[c, x, 8 * g : 8 * g + 8, :], k, 1)
+                first[c % 3] = jnp.where(lane == k, r, first[c % 3])
+                final[c % 3] = jnp.where(lane == (k + 127) % 128, r, final[c % 3])
+        return tuple(first), tuple(final)
+
+    first, final = loop(TX, pack_modes, ((zero,) * 3, (zero,) * 3), TX)
+    for c in range(3):
+        face[0, c] = first[c]
+        face[1, c] = pltpu.roll(final[c], 1, 1)
+
+    face_waits = []
+    for i, o in enumerate(BELOW):
+        face_waits.append(send(o, face.at[0], from_hi.at[-2 * o[0] - o[1]], 11 + i))
+    for i, o in enumerate(SIDES):
+        face_waits.append(send(o, face.at[1], from_side.at[-2 * o[0] - o[1]], 31 + i))
+
+    def shift_modes(x, _):
+        for c in range(6):
+            for g in range(4):
+                rows = slice(8 * g, 8 * g + 8)
+                mz[c, x, rows, :] = pltpu.roll(mb[c, x, rows, :], 127, 1)
+        return 0
+
+    loop(TX, shift_modes, 0, 4)
 
     def clear(ref, index, cond):
         @pl.when(cond)
@@ -320,31 +322,6 @@
         r = pltpu.roll(z_up[f, xb // 2], lax.rem(128 - 4 * k, 128), 1)
         return jnp.where(first_two | last_two, r, 0.0)
 
-    for wait in design_waits:
-        wait()
-    clear_halo(dp, ())
-
-    def put_design(x, g, value):
-        fz[x, 8 * g : 8 * g + 8, :] = value
-
-    sweep(lambda p, a, b: dp[p, a:b, :], put_design, z_out.at[0])
-    z_waits = [send_z(0)]
-
-    for wait in mode_waits:
-        wait()
-    clear(mb, (slice(None), TX), mx == cx - 1)
-    clear(mb, (slice(None), slice(None), slice(TY, TY + 8)), my == cy - 1)
-
-    def shift_halo(c, _):
-        for x in range(TX + 1):
-            mz[c, x, TY : TY + 8, :] = pltpu.roll(mb[c, x, TY : TY + 8, :], 127, 1)
-        for g in range(4):
-            rows = slice(8 * g, 8 * g + 8)
-            mz[c, TX, rows, :] = pltpu.roll(mb[c, TX, rows, :], 127, 1)
-        return 0
-
-    loop(6, shift_halo, 0, 2)
-
     factor = 1.0 / (1.3 * 0.4)
     lam, mu = 0.3 * factor, 0.2 * factor
 
@@ -370,45 +347,43 @@
 
         q0 = s[0, 0, 0, 0] + s[1, 0, 0, 0] + s[2, 0, 0, 0]
         axial = s[0, 1, 0, 0] + s[1, 0, 1, 0] + s[2, 0, 0, 1]
-        q1 = axial + (
+        slide = (
             (s[0, 0, 1, 0] + s[0, 0, 0, 1])
             + (s[1, 1, 0, 0] + s[1, 0, 0, 1])
             + (s[2, 1, 0, 0] + s[2, 0, 1, 0])
         )
+        q1 = axial + slide
         bend = (
             (s[0, 1, 1, 0] + s[0, 1, 0, 1])
             + (s[1, 1, 1, 0] + s[1, 0, 1, 1])
             + (s[2, 1, 0, 1] + s[2, 0, 1, 1])
         )
-        q2 = bend + (s[0, 0, 1, 1] + s[1, 1, 0, 1] + s[2, 1, 1, 0])
+        twist = s[0, 0, 1, 1] + s[1, 1, 0, 1] + s[2, 1, 1, 0]
+        q2 = bend + twist
         q3 = s[0, 1, 1, 1] + s[1, 1, 1, 1] + s[2, 1, 1, 1]
         mass = (1 / 64) * q0 + (1 / 192) * q1 + ((1 / 576) * q2 + (1 / 1728) * q3)
         trace = sq(a[0, 1, 0, 0] + a[1, 0, 1, 0] + a[2, 0, 0, 1])
-        shear = (
-            sq(a[0, 0, 1, 0] + a[1, 1, 0, 0])
-            + sq(a[1, 0, 0, 1] + a[2, 0, 1, 0])
-            + sq(a[0, 0, 0, 1] + a[2, 1, 0, 0])
-        )
-        trace_1 = (
-            sq(a[0, 1, 1, 0] + a[2, 0, 1, 1])
-            + sq(a[0, 1, 0, 1] + a[1, 0, 1, 1])
-            + sq(a[1, 1, 1, 0] + a[2, 1, 0, 1])
-        )
-        shear_1 = (
-            sq(a[0, 0, 1, 1] + a[1, 1, 0, 1])
-            + sq(a[1, 1, 0, 1] + a[2, 1, 1, 0])
-            + sq(a[0, 0, 1, 1] + a[2, 1, 1, 0])
-        )
+        cross = (
+            a[0, 0, 1, 0] * a[1, 1, 0, 0]
+            + a[1, 0, 0, 1] * a[2, 0, 1, 0]
+            + a[0, 0, 0, 1] * a[2, 1, 0, 0]
+        )
+        cross_1 = (
+            a[0, 1, 1, 0] * a[2, 0, 1, 1]
+            + a[0, 1, 0, 1] * a[1, 0, 1, 1]
+            + a[1, 1, 1, 0] * a[2, 1, 0, 1]
+        )
+        shear_1 = sq(a[0, 0, 1, 1] + a[1, 1, 0, 1] + a[2, 1, 1, 0]) + twist
         stiff = (
-            ((lam / 16) * trace + (mu / 8) * axial)
-            + ((mu / 16) * shear + (lam / 48) * trace_1)
-            + ((mu / 16) * bend + (mu / 48) * shear_1)
+            ((lam / 16) * trace + (mu / 8) * (axial + cross))
+            + ((mu / 16) * slide + (lam / 24) * cross_1)
+            + ((mu / 16 + lam / 48) * bend + (mu / 48) * shear_1)
             + ((lam + 4 * mu) / 144) * q3
         )
         return stiff, mass
 
-    def element_pass(m, _):
-        for pairs in range(2):
+    def element_pass(spans, m, _):
+        for pairs, x_from, x_to in spans:
             groups = (2 * pairs, 2 * pairs + 1)
 
             def body(x, held):
@@ -423,11 +398,38 @@
 
             first = []
             for g in groups:
-                first += sum((plane(3 * m + c, 0, g) for c in range(3)), ())
-            lax.fori_loop(0, TX, body, tuple(first))
+                first += sum((plane(3 * m + c, x_from, g) for c in range(3)), ())
+            lax.fori_loop(x_from, x_to, body, tuple(first))
         return 0
 
-    lax.fori_loop(0, 2, element_pass, 0)
+    lax.fori_loop(0, 2, functools.partial(element_pass, ((0, 0, TX - 1),)), 0)
+
+    for wait in design_waits:
+        wait()
+    clear_halo(dp, ())
+
+    def put_design(x, g, value):
+        fz[x, 8 * g : 8 * g + 8, :] = value
+
+    sweep(lambda p, a, b: dp[p, a:b, :], put_design, z_out.at[0])
+    z_waits = [send_z(0)]
+
+    for wait in mode_waits:
+        wait()
+    clear(mb, (slice(None), TX), mx == cx - 1)
+    clear(mb, (slice(None), slice(None), slice(TY, TY + 8)), my == cy - 1)
+
+    def shift_halo(c, _):
+        for x in range(TX + 1):
+            mz[c, x, TY : TY + 8, :] = pltpu.roll(mb[c, x, TY : TY + 8, :], 127, 1)
+        for g in range(4):
+            rows = slice(8 * g, 8 * g + 8)
+            mz[c, TX, rows, :] = pltpu.roll(mb[c, TX, rows, :], 127, 1)
+        return 0
+
+    loop(6, shift_halo, 0, 2)
+
+    lax.fori_loop(0, 2, functools.partial(element_pass, ((0, TX - 1, TX), (1, 0, TX))), 0)
 
     for wait in face_waits:
         wait()
@@ -558,6 +560,7 @@
     def vmem(*shape):
         return pltpu.VMEM(shape, F32)
 
+    arguments = (design, modes.reshape(6, TX, TY, TZ), eigenvalues)
     raw, scale = pl.pallas_call(
         lambda *refs: kernel(sizes, *refs),
         out_shape=(
@@ -595,10 +598,10 @@
             dma((34,)),
         ],
         compiler_params=pltpu.CompilerParams(
-            collective_id=0, has_side_effects=True, vmem_limit_bytes=62 * 1024 * 1024
+            collective_id=0, has_side_effects=True, vmem_limit_bytes=24 * 1024 * 1024
         ),
-    )(design, modes.reshape(6, TX, TY, TZ), eigenvalues)
-    return raw * scale[:, :1, None, None]
+    )(*(pltpu.with_memory_space_constraint(v, pltpu.HBM) for v in arguments))
+    return raw * scale[:, None, None, :]
 
 
 def solution(mesh):

time: 34.4 us -> 30.9 us (0.90)
  Pallas kernels: 31.5 us -> 29.9 us
  other arithmetic: 1.96 us -> 0.83 us
  local copies, waits for them, and re-layouts: 0.8 us -> 0 us
    pallas_call x1, Pallas kernels: 31.5 us -> 29.9 us  [per_device(): pl.pallas_call(lambda *refs: kernel(sizes, *refs), out_shape=(jax.ShapeDt...]
    mul x1, other arithmetic: 1.96 us -> 0.83 us  [per_device(): return raw * scale[:, None, None, :]]
    slice x1 -> x0, local copies, waits for them, and re-layouts: 0.8 us -> none  [per_device(): return raw * scale[:, :1, None, None]]
where the time goes in v5:
time: 30.9 us; the launch traced here: 30.8 us
  Pallas kernels  29.9 us (97%)
  other arithmetic  0.83 us (3%)
    pallas_call x1, Pallas kernels, per_device(): pl.pallas_call(lambda *refs: kernel(sizes, *refs), out_shape=(jax.ShapeDt...  29.9 us
    mul x1, other arithmetic, per_device(): return raw * scale[:, None, None, :]  0.83 us

profile of v5, /device:TPU:1, one launch (start us, length us, event | category | flops | bytes accessed | tf_op | source)
XLA Modules:
  0.0 30.8 jit_solution(6014061992978087364)
XLA Ops:
  0.0 29.9 %shard_map.37 = (f32[2,16,32,128]{3,2,1,0:T(8,128)S(1)}, f32[2,128]{1,0:T(2,128)S(1)}) custom-call(f32[16,32,128]{2,1,0:T(8,128)} %refs_0_.1, f32[6,16,32,128]{3,2,1,0:T(8,128)} %bitcast.1, f32[2]{0:T(128)} %refs_2_.1), custom_call_target="tpu_custom_call" | custom-call | tf_op jit(solution)/shard_map/pallas_call | solution.py:564
  29.9 0.8 %broadcast_multiply_fusion = f32[2,16,32,128]{3,2,1,0:T(8,128)} fusion(f32[2,16,32,128]{3,2,1,0:T(8,128)S(1)} %get-tuple-element.7, f32[2,128]{1,0:T(2,128)S(1)} %get-tuple-element.8), kind=kLoop, calls=%fused_computation | loop fusion | flops 131072 | bytes 1049600 | tf_op jit(solution)/shard_map/mul | solution.py:604

commit v6 on v5

--- a/solution.py
+++ b/solution.py
@@ -60,6 +60,8 @@
     edge,
     wparts,
     fz,
+    slopes,
+    cubics,
     stiffs,
     mass_terms,
     gp,
@@ -117,8 +119,10 @@
         greet(b_device(lax.rem(b_slot + k, b_count)))
         return 0
 
-    lax.fori_loop(1, a_count, greet_a, 0)
-    lax.fori_loop(1, b_count, greet_b, 0)
+    for k in range(1, a_count):
+        greet_a(k, 0)
+    for k in range(1, b_count):
+        greet_b(k, 0)
 
     heard = a_count - 1 + b_count - 1
     for o in FLAT + [(0, 0, 1), (0, 0, -1)] + BELOW[1:]:
@@ -461,6 +465,20 @@
     edge[0], edge[1] = energies(now, later)
     last = lane >= 127
 
+    def patch_last(xb, _):
+        for i in range(4):
+            for g in range(4):
+                x, rows = 4 * xb + i, slice(8 * g, 8 * g + 8)
+                for m in range(2):
+                    turn = lax.rem(255 - (64 * m + 4 * x + g), 128)
+                    for q, ref in enumerate((stiffs, mass_terms)):
+                        ref[m, x, rows, :] = jnp.where(
+                            last, pltpu.roll(edge[q], turn, 1), ref[m, x, rows, :]
+                        )
+        return 0
+
+    lax.fori_loop(0, 4, patch_last, 0)
+
     top_t = math.tanh(4.0)
     merge_z(0, z_waits[0])
     eigs = [eig[m] for m in range(2)]
@@ -477,16 +495,10 @@
                 inverse = 1.0 / (wparts[0, g] + x1 * wparts[1, g] + x2 * wparts[2, g])
                 t = jnp.tanh(8.0 * ((fz[x, rows, :] + from_z(0, xb, i, g)) * inverse - 0.5))
                 rho = (top_t + t) * (0.5 / top_t)
-                slope = (1.0 - t * t) * inverse * (4.0 / top_t)
-                cubic = (3.0 * (1.0 - 0.001)) * (rho * rho)
+                slopes[x, rows, :] = (1.0 - t * t) * inverse * (4.0 / top_t)
+                cubics[x, rows, :] = (3.0 * (1.0 - 0.001)) * (rho * rho)
                 for m in range(2):
-                    turn = lax.rem(255 - (64 * m + 4 * x + g), 128)
-                    mass = jnp.where(last, pltpu.roll(edge[1], turn, 1), mass_terms[m, x, rows, :])
-                    stiff = jnp.where(last, pltpu.roll(edge[0], turn, 1), stiffs[m, x, rows, :])
-                    acc[m] = acc[m] + rho * mass
-                    gp[m, x + 2, 8 + 8 * g : 16 + 8 * g, :] = (
-                        cubic * stiff - eigs[m] * mass
-                    ) * slope
+                    acc[m] = acc[m] + rho * mass_terms[m, x, rows, :]
         return tuple(acc)
 
     masses = lax.fori_loop(0, 4, project, (zero, zero))
@@ -501,10 +513,24 @@
 
             return 0
 
-        lax.fori_loop(0, count, start, 0)
+        for k in range(count):
+            start(k, 0)
         return remote(ref.at[pl.ds(0, count - 1)], ref.at[pl.ds(0, count - 1)], sem, me)
 
     a_copies = spread_sum(a_in, a_count, a_slot, a_device, 29)
+
+    def gradients(xb, _):
+        for i in range(4):
+            for g in range(4):
+                x, rows = 4 * xb + i, slice(8 * g, 8 * g + 8)
+                for m in range(2):
+                    gp[m, x + 2, 8 + 8 * g : 16 + 8 * g, :] = (
+                        cubics[x, rows, :] * stiffs[m, x, rows, :]
+                        - eigs[m] * mass_terms[m, x, rows, :]
+                    ) * slopes[x, rows, :]
+        return 0
+
+    lax.fori_loop(0, 4, gradients, 0)
     flats = send_flats(gp, gp, (slice(None),), (2, 8), 15)
 
     for wait in flats:
@@ -518,10 +544,10 @@
 
         sweep(lambda p, a, b, m=m: gp[m, p, a:b, :], put_grad, z_out.at[1 + m])
         z_waits.append(send_z(1 + m))
-
-    a_copies.wait_recv()
-    b_in[b_slot] = jnp.sum(a_in[...], axis=0)
-    b_copies = spread_sum(b_in, b_count, b_slot, b_device, 30)
+        if m == 0:
+            a_copies.wait_recv()
+            b_in[b_slot] = jnp.sum(a_in[...], axis=0)
+            b_copies = spread_sum(b_in, b_count, b_slot, b_device, 30)
 
     for m in range(2):
         merge_z(1 + m, z_waits[1 + m])
@@ -540,16 +566,15 @@
         store.start()
         stores.append(store)
 
+    for wait in sent:
+        wait()
+    a_copies.wait_send()
+    for store in stores:
+        store.wait()
     b_copies.wait_recv()
     total = jnp.sum(jnp.sum(b_in[...], axis=0), axis=1, keepdims=True)
     scale_ref[...] = jnp.broadcast_to(count / total, (2, 128))
-
-    for wait in sent:
-        wait()
-    a_copies.wait_send()
     b_copies.wait_send()
-    for store in stores:
-        store.wait()
 
 
 def per_device(sizes, design, modes, eigenvalues):
@@ -582,6 +607,8 @@
             vmem(2, 8, 128),
             vmem(3, 4, 8, 128),
             vmem(TX, TY, TZ),
+            vmem(TX, TY, TZ),
+            vmem(TX, TY, TZ),
             vmem(2, TX, TY, TZ),
             vmem(2, TX, TY, TZ),
             vmem(2, TX + 4, TY + 16, TZ),

time: 30.9 us -> 30.1 us (0.974)
  Pallas kernels: 29.9 us -> 29.2 us
    pallas_call x1, Pallas kernels: 29.9 us -> 29.2 us  [per_device(): pl.pallas_call(lambda *refs: kernel(sizes, *refs), out_shape=(jax.ShapeDt...]
where the time goes in v6:
time: 30.1 us; the launch traced here: 30 us
  Pallas kernels  29.2 us (97%)
  other arithmetic  0.83 us (3%)
    pallas_call x1, Pallas kernels, per_device(): pl.pallas_call(lambda *refs: kernel(sizes, *refs), out_shape=(jax.ShapeDt...  29.2 us
    mul x1, other arithmetic, per_device(): return raw * scale[:, None, None, :]  0.83 us

profile of v6, /device:TPU:1, one launch (start us, length us, event | category | flops | bytes accessed | tf_op | source)
XLA Modules:
  0.0 30.0 jit_solution(836526419787840243)
XLA Ops:
  0.0 29.2 %shard_map.37 = (f32[2,16,32,128]{3,2,1,0:T(8,128)S(1)}, f32[2,128]{1,0:T(2,128)S(1)}) custom-call(f32[16,32,128]{2,1,0:T(8,128)} %refs_0_.1, f32[6,16,32,128]{3,2,1,0:T(8,128)} %bitcast.1, f32[2]{0:T(128)} %refs_2_.1), custom_call_target="tpu_custom_call" | custom-call | tf_op jit(solution)/shard_map/pallas_call | solution.py:589
  29.2 0.8 %broadcast_multiply_fusion = f32[2,16,32,128]{3,2,1,0:T(8,128)} fusion(f32[2,16,32,128]{3,2,1,0:T(8,128)S(1)} %get-tuple-element.7, f32[2,128]{1,0:T(2,128)S(1)} %get-tuple-element.8), kind=kLoop, calls=%fused_computation | loop fusion | flops 131072 | bytes 1049600 | tf_op jit(solution)/shard_map/mul | solution.py:631

commit v7 on v6

--- a/solution.py
+++ b/solution.py
@@ -503,7 +503,7 @@
 
     masses = lax.fori_loop(0, 4, project, (zero, zero))
     for m in range(2):
-        a_in[a_slot, m : m + 1, :] = jnp.sum(masses[m], axis=0, keepdims=True)
+        b_in[b_slot, m : m + 1, :] = jnp.sum(masses[m], axis=0, keepdims=True)
 
     def spread_sum(ref, count, slot, device, sem):
         def start(k, _):
@@ -517,7 +517,7 @@
             start(k, 0)
         return remote(ref.at[pl.ds(0, count - 1)], ref.at[pl.ds(0, count - 1)], sem, me)
 
-    a_copies = spread_sum(a_in, a_count, a_slot, a_device, 29)
+    b_copies = spread_sum(b_in, b_count, b_slot, b_device, 30)
 
     def gradients(xb, _):
         for i in range(4):
@@ -545,9 +545,9 @@
         sweep(lambda p, a, b, m=m: gp[m, p, a:b, :], put_grad, z_out.at[1 + m])
         z_waits.append(send_z(1 + m))
         if m == 0:
-            a_copies.wait_recv()
-            b_in[b_slot] = jnp.sum(a_in[...], axis=0)
-            b_copies = spread_sum(b_in, b_count, b_slot, b_device, 30)
+            b_copies.wait_recv()
+            a_in[a_slot] = jnp.sum(b_in[...], axis=0)
+            a_copies = spread_sum(a_in, a_count, a_slot, a_device, 29)
 
     for m in range(2):
         merge_z(1 + m, z_waits[1 + m])
@@ -568,13 +568,13 @@
 
     for wait in sent:
         wait()
-    a_copies.wait_send()
+    b_copies.wait_send()
     for store in stores:
         store.wait()
-    b_copies.wait_recv()
-    total = jnp.sum(jnp.sum(b_in[...], axis=0), axis=1, keepdims=True)
+    a_copies.wait_recv()
+    total = jnp.sum(jnp.sum(a_in[...], axis=0), axis=1, keepdims=True)
     scale_ref[...] = jnp.broadcast_to(count / total, (2, 128))
-    b_copies.wait_send()
+    a_copies.wait_send()
 
 
 def per_device(sizes, design, modes, eigenvalues):

time: 30.1 us -> 29.5 us (0.980)
  Pallas kernels: 29.2 us -> 28.6 us
    pallas_call x1, Pallas kernels: 29.2 us -> 28.6 us  [per_device(): pl.pallas_call(lambda *refs: kernel(sizes, *refs), out_shape=(jax.ShapeDt...]
where the time goes in v7:
time: 29.5 us; the launch traced here: 29.4 us
  Pallas kernels  28.6 us (97%)
  other arithmetic  0.83 us (3%)
    pallas_call x1, Pallas kernels, per_device(): pl.pallas_call(lambda *refs: kernel(sizes, *refs), out_shape=(jax.ShapeDt...  28.6 us
    mul x1, other arithmetic, per_device(): return raw * scale[:, None, None, :]  0.83 us

profile of v7, /device:TPU:1, one launch (start us, length us, event | category | flops | bytes accessed | tf_op | source)
XLA Modules:
  0.0 29.4 jit_solution(7352068644830924446)
XLA Ops:
  0.0 28.6 %shard_map.37 = (f32[2,16,32,128]{3,2,1,0:T(8,128)S(1)}, f32[2,128]{1,0:T(2,128)S(1)}) custom-call(f32[16,32,128]{2,1,0:T(8,128)} %refs_0_.1, f32[6,16,32,128]{3,2,1,0:T(8,128)} %bitcast.1, f32[2]{0:T(128)} %refs_2_.1), custom_call_target="tpu_custom_call" | custom-call | tf_op jit(solution)/shard_map/pallas_call | solution.py:589
  28.6 0.8 %broadcast_multiply_fusion = f32[2,16,32,128]{3,2,1,0:T(8,128)} fusion(f32[2,16,32,128]{3,2,1,0:T(8,128)S(1)} %get-tuple-element.7, f32[2,128]{1,0:T(2,128)S(1)} %get-tuple-element.8), kind=kLoop, calls=%fused_computation | loop fusion | flops 131072 | bytes 1049600 | tf_op jit(solution)/shard_map/mul | solution.py:631
